TPU v7x, 32 devices: a whole 2x2x4 slice. The times are simulated.
32 devices in a mesh: groups: 2 (over x), ctx: 16 (over z, y, core).
Axes of the slice: x: 2, y: 2, z: 4, core: 2. Of those that a mesh axis runs over, the one named last changes fastest.
Arguments:
- conv_input: bfloat16 [4096, 2176], P(('groups', 'ctx')), parts along dimension 0, may hold values from -6 to 6
- conv_weight: float32 [4, 2176], replicated, may hold values from -3 to 3
- log_decay: float32 [32, 4096], P(None, ('groups', 'ctx')), parts along dimension 1, may hold values from -6 to 0
- level_weight: float32 [12, 32, 4096], P(None, None, ('groups', 'ctx')), parts along dimension 2, may hold values from 0.5 to 2
- grad_out: bfloat16 [4096, 2048], P(('groups', 'ctx')), parts along dimension 0, may hold values from -1.5 to 1.5
Outputs:
- mixed: bfloat16 [4096, 2048], P(('groups', 'ctx')), parts along dimension 0
- grad_input: bfloat16 [4096, 2176], P(('groups', 'ctx')), parts along dimension 0
- grad_level: float32 [12, 32, 4096], P(None, None, ('groups', 'ctx')), parts along dimension 2
- grad_conv: float32 [8, 2176], P('groups'), parts along dimension 0
There are 2 independent parts, one for each index of `groups`. A program takes and returns all parts, laid end to end along the dimension named above; an argument that names none is the same for every part. Nothing has to cross between parts.
All inputs are finite; a program needn't handle non-finite values.
Results may differ from a plain program's by a relative error of at most 0.005.
Values may be sent and summed in bfloat16 or wider, within the bound.
A program may use at most 128 MiB of HBM per device.

v0:
```python
import functools

import jax
import jax.numpy as jnp
from jax import lax
from jax.experimental import pallas as pl
from jax.experimental.pallas import tpu as pltpu
from jax.sharding import PartitionSpec as P

BLOCK = 64
LANES = 128
MESH = pl.DeviceIdType.MESH
HIGH = lax.Precision.HIGHEST
F32 = jnp.float32
BF16 = jnp.bfloat16
VMEM_LIMIT = 56 * 1024 * 1024


def level_scale(level_idx):
    if level_idx == 0:
        return BLOCK**-0.5
    return (BLOCK * 2 ** (level_idx - 1)) ** -0.5


def dot(a, b):
    return jnp.dot(a, b, preferred_element_type=F32)


def dot_nt(a, b):
    return lax.dot_general(a, b, (((1,), (1,)), ((), ())), preferred_element_type=F32)


def split2(v):
    hi = v.astype(BF16)
    return hi, (v - hi.astype(F32)).astype(BF16)


def split3(v):
    hi = v.astype(BF16)
    rest = v - hi.astype(F32)
    mid = rest.astype(BF16)
    return hi, mid, (rest - mid.astype(F32)).astype(BF16)


def iota(shape, axis):
    return lax.broadcasted_iota(jnp.int32, shape, axis)


def one_hot(rows, heads, first, lanes, width):
    return jnp.where(
        iota((rows, lanes), 0) % heads == first + iota((rows, lanes), 1) // width, 1.0, 0.0
    ).astype(BF16)


def greet(peers):
    barrier = pltpu.get_barrier_semaphore()
    for peer in peers:
        pl.semaphore_signal(barrier, inc=1, device_id=peer, device_id_type=MESH)
    pl.semaphore_wait(barrier, len(peers))


def at(peer):
    return (lax.axis_index("groups"), peer)


def edge_kernel(n, conv_ref, decay_ref, prior_ref, totals_ref, mine, slots, rows, send, recv, rsend, rrecv):
    me = lax.axis_index("ctx")
    peers = [lax.rem(me + d, n) for d in range(1, n)]
    heads = decay_ref.shape[0]
    mine[...] = jnp.zeros_like(mine)
    mine[:, :heads] = lax.dot_general(
        jnp.ones((8, decay_ref.shape[1]), F32),
        decay_ref[...],
        (((1,), (1,)), ((), ())),
        precision=HIGH,
        preferred_element_type=F32,
    )
    greet([at(p) for p in peers])
    copies = []
    count = conv_ref.shape[0]
    row_copy = pltpu.make_async_remote_copy(
        conv_ref.at[pl.ds(count - 16, 16), :], rows, rsend, rrecv, at(peers[0]), MESH
    )
    row_copy.start()
    for d in range(1, n):
        copy = pltpu.make_async_remote_copy(
            mine, slots.at[d - 1], send.at[d - 1], recv.at[d - 1], at(peers[d - 1]), MESH
        )
        copy.start()
        copies.append(copy)
    totals_ref[me] = mine[...]
    for d in range(1, n):
        copies[d - 1].wait()
        totals_ref[lax.rem(me - d + n, n)] = slots[d - 1]
    row_copy.wait()
    keep = jnp.where(me > 0, 1.0, 0.0)
    prior_ref[...] = (rows[...].astype(F32) * keep).astype(BF16)


def exchange_edges(n, conv_input, log_decay):
    channels = conv_input.shape[1]
    vm = pl.BlockSpec(memory_space=pltpu.VMEM)
    return pl.pallas_call(
        functools.partial(edge_kernel, n),
        out_shape=(
            jax.ShapeDtypeStruct((16, channels), BF16),
            jax.ShapeDtypeStruct((n, 8, LANES), F32),
        ),
        in_specs=[vm, vm],
        out_specs=(vm, vm),
        scratch_shapes=[
            pltpu.VMEM((8, LANES), F32),
            pltpu.VMEM((n - 1, 8, LANES), F32),
            pltpu.VMEM((16, channels), BF16),
            pltpu.SemaphoreType.DMA((n - 1,)),
            pltpu.SemaphoreType.DMA((n - 1,)),
            pltpu.SemaphoreType.DMA,
            pltpu.SemaphoreType.DMA,
        ],
        compiler_params=pltpu.CompilerParams(
            collective_id=0, has_side_effects=True, vmem_limit_bytes=VMEM_LIMIT
        ),
    )(conv_input, log_decay)


def fill_padded(pad, conv_ref, prior_ref):
    pad[0:8, :] = prior_ref[...].astype(F32)[8:16]
    pad[8:, :] = conv_ref[...].astype(F32)


def running_decay(decay_ref):
    rows = decay_ref.shape[1]
    lower = jnp.where(iota((rows, rows), 0) >= iota((rows, rows), 1), 1.0, 0.0)
    by_token = jnp.dot(lower, decay_ref[...].T, precision=HIGH, preferred_element_type=F32)
    return by_token


def front_kernel(
    far, conv_ref, prior_ref, w_ref, decay_ref, lw_ref, g_ref, totals_ref,
    u_ref, slope_ref, end_ref, gf_ref, fac_ref, pad, facs,
):
    me = lax.axis_index("ctx")
    rows, channels = g_ref.shape
    heads = decay_ref.shape[0]
    taps = w_ref.shape[0]
    fill_padded(pad, conv_ref, prior_ref)
    totals = totals_ref[...][:, 0, :heads]
    spans = iota(totals.shape, 0)

    def span(lo, hi):
        return jnp.sum(jnp.where((spans >= lo) & (spans < hi), totals, 0.0), axis=0, keepdims=True)

    own, pre = [], []
    for level in range(far):
        half = me >> level
        upper = (half & 1) == 1
        start = half << level
        sib = (half ^ 1) << level
        size = 1 << level
        own.append(jnp.exp(jnp.where(upper, 0.0, 1.0) * span(sib, sib + size)))
        own.append(jnp.exp(jnp.where(upper, 1.0, 0.0) * span(start, start + size)))
        pre.append(jnp.where(upper, 1.0, 0.0) * jnp.exp(span(start, me)))
    count = fac_ref.shape[1]
    stack = own + pre
    if count > len(stack):
        stack.append(jnp.zeros((count - len(stack), heads), F32))
    small = jnp.concatenate(split2(jnp.concatenate(stack, axis=0)), axis=1)

    cum = running_decay(decay_ref)
    in_device = jnp.exp(cum)
    base = [jnp.exp(cum[rows - 1 : rows] - cum)]
    for level in range(far):
        base.append(in_device * lw_ref[2 + level].T * (level_scale(2 + level) * pre[level]))
    for idx, value in enumerate(base):
        facs[idx * rows : (idx + 1) * rows, :] = jnp.concatenate(split2(value), axis=1)

    def activate(cols):
        acc = w_ref[0:1, cols] * pad[8 - taps + 1 : 8 - taps + 1 + rows, cols]
        for k in range(1, taps):
            acc = acc + w_ref[k : k + 1, cols] * pad[8 - taps + 1 + k : 8 - taps + 1 + k + rows, cols]
        sig = jax.nn.sigmoid(acc)
        u = (acc * sig).astype(BF16)
        u_ref[:, cols] = u
        slope_ref[:, cols] = sig * (1.0 + acc * (1.0 - sig))
        return u

    bq = activate(pl.ds(channels, LANES)).astype(F32).T.astype(BF16)
    b_t = jnp.concatenate([bq[:BLOCK]] * 2, axis=1)
    q_t = jnp.concatenate([bq[BLOCK:]] * 2, axis=1)
    per_half = channels // 2 // LANES

    @pl.loop(0, channels // LANES)
    def _(j):
        cols = pl.ds(pl.multiple_of(j * LANES, LANES), LANES)
        side = j // per_half
        out = pl.ds(pl.multiple_of((j % per_half) * LANES, LANES), LANES)
        x = activate(cols).astype(F32)
        hot = one_hot(2 * heads, heads, 2 * j, LANES, BLOCK)
        spread = dot(facs[...], hot)
        fac_ref[side, :, out] = dot(small, hot)
        end_ref[side, :, out] = dot(b_t, jnp.concatenate(split2(x * spread[:rows]), axis=0))
        g = g_ref[:, cols].astype(F32)
        for level in range(far):
            inner = g * spread[(1 + level) * rows : (2 + level) * rows]
            gf_ref[level, side, :, out] = dot(q_t, jnp.concatenate(split2(inner), axis=0))


def fenwick_kernel(
    far, end_ref, gf_ref, fac_ref, far_ref, grad_ref,
    up0, up0_in, up, up_in, cross_in, merge, merge_in, down, down_in, last, last_in,
    sems_s, sems_r, run, back,
):
    me = lax.axis_index("ctx")
    core = me & 1
    other = 1 - core
    peers = [at(me ^ (1 << level)) for level in range(far)]

    def copy(src, dst, kind, level, peer):
        made = pltpu.make_async_remote_copy(
            src, dst, sems_s.at[kind, level], sems_r.at[kind, level], peer, MESH
        )
        made.start()
        return made

    pending = []
    up0[...] = end_ref[...].astype(BF16)
    for level in range(1, far):
        merge[level - 1] = gf_ref[level, other].astype(BF16)
    greet(peers)
    merge_copy = copy(merge, merge_in, 0, 0, peers[0])
    up_copy = copy(up0, up0_in, 1, 0, peers[0])
    crosses = []

    def own_coef(level):
        return fac_ref[core, 2 * level : 2 * level + 1, :]

    def sib_coef(level):
        return fac_ref[core, 2 * level + 1 : 2 * level + 2, :]

    merge_copy.wait()
    pending_down = None
    for step in range(far - 1):
        level = far - 1 - step
        total = gf_ref[level, core] + merge_in[level - 1].astype(F32)
        if step > 0:
            pending_down.wait()
            back[...] = back[...] * own_coef(level + 1) if step > 1 else jnp.zeros_like(back)
            back[...] = back[...] + down_in[level].astype(F32)
            total = total + back[...] * sib_coef(level)
        down[level - 1] = total.astype(BF16)
        pending_down = copy(down.at[level - 1], down_in.at[level - 1], 2, level, peers[level])

        up_copy.wait()
        if step == 0:
            run[...] = end_ref[core] * own_coef(0) + up0_in[core].astype(F32) * sib_coef(0)
        else:
            crosses.append(copy(up_in.at[step - 1], cross_in.at[step - 1], 3, step, peers[0]))
            run[...] = run[...] * own_coef(step) + up_in[step - 1].astype(F32) * sib_coef(step)
        up[step] = run[...].astype(BF16)
        up_copy = copy(up.at[step], up_in.at[step], 1, step + 1, peers[step + 1])
    pending_down.wait()
    if far > 2:
        back[...] = back[...] * own_coef(1) + down_in[0].astype(F32)
    else:
        back[...] = down_in[0].astype(F32)
    last[core] = (gf_ref[0, core] + back[...] * sib_coef(0)).astype(BF16)
    last[other] = gf_ref[0, other].astype(BF16)
    last_copy = copy(last, last_in, 4, 0, peers[0])
    up_copy.wait()
    crosses.append(copy(up_in.at[far - 2], cross_in.at[far - 2], 3, far - 1, peers[0]))
    far_ref[0] = up0_in[...]
    for level in range(1, far):
        far_ref[level, core] = up_in[level - 1]
    last_copy.wait()
    grad_ref[core] = back[...] * own_coef(0) + last_in[core].astype(F32)
    grad_ref[other] = last_in[other].astype(F32)
    for level in range(1, far):
        crosses[level - 1].wait()
        far_ref[level, other] = cross_in[level - 1]


def exchange_states(far, end_state, grad_far, factors):
    half = end_state.shape
    piece = half[1:]
    vm = pl.BlockSpec(memory_space=pltpu.VMEM)
    stack = (far - 1,) + piece
    return pl.pallas_call(
        functools.partial(fenwick_kernel, far),
        out_shape=(
            jax.ShapeDtypeStruct((far,) + half, BF16),
            jax.ShapeDtypeStruct(half, F32),
        ),
        in_specs=[vm] * 3,
        out_specs=(vm, vm),
        scratch_shapes=[
            pltpu.VMEM(half, BF16),
            pltpu.VMEM(half, BF16),
            pltpu.VMEM(stack, BF16),
            pltpu.VMEM(stack, BF16),
            pltpu.VMEM(stack, BF16),
            pltpu.VMEM(stack, BF16),
            pltpu.VMEM(stack, BF16),
            pltpu.VMEM(stack, BF16),
            pltpu.VMEM(stack, BF16),
            pltpu.VMEM(half, BF16),
            pltpu.VMEM(half, BF16),
            pltpu.SemaphoreType.DMA((5, far)),
            pltpu.SemaphoreType.DMA((5, far)),
            pltpu.VMEM(piece, F32),
            pltpu.VMEM(piece, F32),
        ],
        compiler_params=pltpu.CompilerParams(
            collective_id=1, has_side_effects=True, vmem_limit_bytes=VMEM_LIMIT
        ),
    )(end_state, grad_far, factors)


def back_kernel(
    far, conv_ref, prior_ref, w_ref, decay_ref, lw_ref, g_ref, u_ref, slope_ref, fac_ref, far_ref, grad_ref,
    mixed_ref, gin_ref, glev_ref, tail_ref, head_ref, wpart_ref,
    pad, gp, facs, cum3, cum_rows, bias, scores, hotx, hotg, q_s, b2_s, ds_acc, dq_acc, db_acc,
):
    rows, channels = g_ref.shape
    heads = decay_ref.shape[0]
    taps = w_ref.shape[0]
    wide = 2 * rows
    fill_padded(pad, conv_ref, prior_ref)
    cum = running_decay(decay_ref)
    cum_rows[...] = cum.T
    cum3[...] = jnp.concatenate(split3(cum), axis=1)
    base = [lw_ref[0].T * level_scale(0), lw_ref[1].T * level_scale(1)]
    base += [jnp.exp(cum[rows - 1 : rows] - cum), jnp.exp(cum)]
    base += [lw_ref[2 + level].T * level_scale(2 + level) for level in range(far)]
    for idx, value in enumerate(base):
        facs[idx * rows : (idx + 1) * rows, :] = jnp.concatenate(split2(value), axis=1)
    first = iota((rows, wide), 0)
    second = iota((rows, wide), 1) % rows
    bias[0] = jnp.where(second <= first, 0.0, -1e30)
    bias[1] = jnp.where(first <= second, 0.0, -1e30)
    r, c = iota((wide, wide), 0), iota((wide, wide), 1)
    same = (r // rows) == (c % LANES) // BLOCK
    block1 = (r % rows) // BLOCK == 1
    hotg[...] = jnp.where(same, 1.0, 0.0).astype(BF16)
    hotx[...] = jnp.where(same & (block1 == (c < LANES)), 1.0, 0.0).astype(BF16)
    bq = u_ref[:, channels:]
    b, q = bq[:, :BLOCK], bq[:, BLOCK:]
    q_s[...] = q
    b2_s[...] = jnp.concatenate([b, b], axis=1)
    scores[0] = dot_nt(q, jnp.concatenate([b, b], axis=0))
    scores[1] = dot_nt(b, jnp.concatenate([q, q], axis=0))
    ds_acc[...] = jnp.zeros_like(ds_acc)
    dq_acc[...] = jnp.zeros_like(dq_acc)
    db_acc[...] = jnp.zeros_like(db_acc)
    glev_ref[...] = jnp.zeros_like(glev_ref)
    per_half = channels // 2 // LANES
    low = iota((rows, LANES), 0) < BLOCK

    @pl.loop(0, channels // LANES)
    def _(j):
        cols = pl.ds(pl.multiple_of(j * LANES, LANES), LANES)
        side = j // per_half
        part = pl.ds(pl.multiple_of((j % per_half) * LANES, LANES), LANES)
        x = u_ref[:, cols]
        g = g_ref[:, cols].astype(F32)
        spread = dot(facs[...], one_hot(2 * heads, heads, 2 * j, LANES, BLOCK))

        def fac(idx):
            return spread[idx * rows : (idx + 1) * rows]

        w0, w1 = fac(0), fac(1)
        col = dot(cum3[...], one_hot(3 * heads, heads, 2 * j, wide, rows))
        row = jnp.concatenate([cum_rows[pl.ds(2 * j, 1), :], cum_rows[pl.ds(2 * j + 1, 1), :]], axis=1)
        gap = col - row
        decay = jnp.exp(gap + bias[0])
        mix = (scores[0] * decay).astype(BF16)
        mix_t = (scores[1] * jnp.exp(bias[1] - gap)).astype(BF16)
        wx = jnp.concatenate([jnp.concatenate([x, x], axis=1)] * 2, axis=0) * hotx[...]
        res = dot(mix, wx)
        out0 = jnp.where(low, res[:, LANES:], res[:, :LANES])
        out1 = jnp.where(low, 0.0, res[:, LANES:])
        gz = (g * w0).astype(BF16)
        gh = (g * jnp.where(low, w0, w1)).astype(BF16)
        gg = jnp.concatenate([gz, gh], axis=1)
        ds_acc[...] += decay * dot_nt(gg, wx)
        res = dot(mix_t, jnp.concatenate([gg, gg], axis=0) * hotg[...])
        dx = jnp.where(low, res[:, LANES:], res[:, :LANES])

        mixed = w0 * out0 + w1 * out1
        products = [g * out0, g * out1]
        inner, states = [], []
        for level in range(far):
            state = far_ref[level, side, :, part]
            scale = fac(3) * fac_ref[side, 2 * far + level : 2 * far + level + 1, part]
            out = dot(q_s[...], state) * scale
            weight = fac(4 + level)
            mixed = mixed + weight * out
            products.append(g * out)
            inner.append((g * weight * scale).astype(BF16))
            states.append(state)
        mixed_ref[:, cols] = mixed.astype(BF16)
        dq_acc[...] += dot_nt(jnp.concatenate(inner, axis=1), jnp.concatenate(states, axis=1))
        pick = jnp.where(
            iota((heads, 2 * LANES), 0) == 2 * j + (iota((heads, 2 * LANES), 1) % LANES) // BLOCK, 1.0, 0.0
        ).astype(BF16)
        for level, product in enumerate(products):
            glev_ref[level] += dot_nt(pick, jnp.concatenate(split2(product), axis=1)) * level_scale(level)

        grad = grad_ref[side, :, part]
        hi, lo = split2(grad)
        key_decay = fac(2)
        dx = dx + key_decay * dot(b2_s[...], jnp.concatenate([hi, lo], axis=0))
        db_acc[...] += dot_nt((x.astype(F32) * key_decay).astype(BF16), hi)
        gp[0:rows, cols] = dx * slope_ref[:, cols]

    ds = ds_acc[:, :rows] + ds_acc[:, rows:]
    dq = dq_acc[...] + dot(ds.astype(BF16), b)
    db = db_acc[...] + dot(ds.T.astype(BF16), q)
    gp[0:rows, channels:] = jnp.concatenate([db, dq], axis=1) * slope_ref[:, channels:]
    gp[rows:, :] = jnp.zeros((8, gp.shape[1]), F32)
    head_ref[...] = gp[0:8, :]

    @pl.loop(0, gp.shape[1] // LANES)
    def _(j):
        cols = pl.ds(pl.multiple_of(j * LANES, LANES), LANES)
        grad = gp[0:rows, cols]
        acc = w_ref[taps - 1 : taps, cols] * grad
        sums = []
        for k in range(taps):
            shift = taps - 1 - k
            if shift:
                acc = acc + w_ref[k : k + 1, cols] * gp[shift : shift + rows, cols]
            sums.append(jnp.sum(pad[8 - shift : 8 - shift + rows, cols] * grad, axis=0, keepdims=True))
        gin_ref[:, cols] = acc.astype(BF16)
        tail_ref[:, cols] = acc[rows - 16 :]
        sums.append(jnp.zeros((8 - taps, LANES), F32))
        wpart_ref[:, cols] = jnp.concatenate(sums, axis=0)


def finish_kernel(n, digits, tail_ref, head_ref, wpart_ref, w_ref, out_ref, wsum_ref, nxt, acc, slots, hs, hr, send, recv):
    me = lax.axis_index("ctx")
    taps = w_ref.shape[0]
    before, after = lax.rem(me + n - 1, n), lax.rem(me + 1, n)
    plan = []
    for shift, size in digits:
        digit = (me >> shift) & (size - 1)
        plan.append((digit, [me ^ (d << shift) for d in range(1, size)]))
    greet([at(before), at(after)] + [at(p) for _, peers in plan for p in peers])
    row_copy = pltpu.make_async_remote_copy(head_ref, nxt, hs, hr, at(before), MESH)
    row_copy.start()
    acc[0] = wpart_ref[...]
    for stage, (digit, peers) in enumerate(plan):
        copies = []
        for d, peer in enumerate(peers):
            copy = pltpu.make_async_remote_copy(
                acc.at[stage], slots.at[stage, d], send.at[stage, d], recv.at[stage, d], at(peer), MESH
            )
            copy.start()
            copies.append(copy)
        if stage == 0:
            row_copy.wait()
            keep = jnp.where(me < n - 1, 1.0, 0.0)
            rows = nxt[...] * keep
            joined = jnp.concatenate([jnp.zeros((8, rows.shape[1]), F32), rows], axis=0)
            fix = jnp.zeros((8, rows.shape[1]), F32)
            for k in range(taps - 1):
                shift = taps - 1 - k
                fix = fix + w_ref[k : k + 1, :] * joined[shift : shift + 8]
            out_ref[...] = (tail_ref[...] + jnp.concatenate([jnp.zeros_like(fix), fix], axis=0)).astype(BF16)
        for copy in copies:
            copy.wait()
        size = len(peers) + 1
        have = [acc[stage]] + [slots[stage, d] for d in range(size - 1)]
        if size == 2:
            total = have[0] + have[1]
        else:
            total = (have[0] + have[1]) + (have[2] + have[3])
        acc[stage + 1] = total
    wsum_ref[...] = acc[len(plan)][:taps]


def exchange_finish(n, tail, head, wpart, conv_weight):
    far = n.bit_length() - 1
    digits = []
    shift = 0
    while shift < far:
        bits = min(2, far - shift)
        digits.append((shift, 1 << bits))
        shift += bits
    channels = tail.shape[1]
    vm = pl.BlockSpec(memory_space=pltpu.VMEM)
    return pl.pallas_call(
        functools.partial(finish_kernel, n, digits),
        out_shape=(
            jax.ShapeDtypeStruct((16, channels), BF16),
            jax.ShapeDtypeStruct(conv_weight.shape, F32),
        ),
        in_specs=[vm] * 4,
        out_specs=(vm, vm),
        scratch_shapes=[
            pltpu.VMEM((8, channels), F32),
            pltpu.VMEM((len(digits) + 1, 8, channels), F32),
            pltpu.VMEM((len(digits), 3, 8, channels), F32),
            pltpu.SemaphoreType.DMA,
            pltpu.SemaphoreType.DMA,
            pltpu.SemaphoreType.DMA((len(digits), 3)),
            pltpu.SemaphoreType.DMA((len(digits), 3)),
        ],
        compiler_params=pltpu.CompilerParams(
            collective_id=2, has_side_effects=True, vmem_limit_bytes=VMEM_LIMIT
        ),
    )(tail, head, wpart, conv_weight)


def body(conv_input, conv_weight, log_decay, level_weight, grad_out):
    n = lax.axis_size("ctx")
    far = n.bit_length() - 1
    rows, conv_ch = conv_input.shape
    channels = grad_out.shape[1]
    heads = log_decay.shape[0]
    vm = pl.BlockSpec(memory_space=pltpu.VMEM)
    params = pltpu.CompilerParams(vmem_limit_bytes=VMEM_LIMIT)
    shape = jax.ShapeDtypeStruct
    half = (2, BLOCK, channels // 2)
    fac_rows = (3 * far + 7) // 8 * 8
    prior, totals = exchange_edges(n, conv_input, log_decay)
    u_act, slope, end_state, grad_far, factors = pl.pallas_call(
        functools.partial(front_kernel, far),
        out_shape=(
            shape((rows, conv_ch), BF16),
            shape((rows, conv_ch), F32),
            shape(half, F32),
            shape((far,) + half, F32),
            shape((2, fac_rows, channels // 2), F32),
        ),
        in_specs=[vm] * 7,
        out_specs=(vm,) * 5,
        scratch_shapes=[
            pltpu.VMEM((rows + 8, conv_ch), F32),
            pltpu.VMEM(((1 + far) * rows, 2 * heads), BF16),
        ],
        compiler_params=params,
    )(conv_input, prior, conv_weight, log_decay, level_weight, grad_out, totals)
    far_states, grad_end = exchange_states(far, end_state, grad_far, factors)
    mixed, grad_input, grad_level, tail, head, wpart = pl.pallas_call(
        functools.partial(back_kernel, far),
        out_shape=(
            shape((rows, channels), BF16),
            shape((rows, conv_ch), BF16),
            shape(level_weight.shape, F32),
            shape((16, conv_ch), F32),
            shape((8, conv_ch), F32),
            shape((8, conv_ch), F32),
        ),
        in_specs=[vm] * 11,
        out_specs=(vm,) * 6,
        scratch_shapes=[
            pltpu.VMEM((rows + 8, conv_ch), F32),
            pltpu.VMEM((rows + 8, conv_ch), F32),
            pltpu.VMEM(((4 + far) * rows, 2 * heads), BF16),
            pltpu.VMEM((rows, 3 * heads), BF16),
            pltpu.VMEM((heads, rows), F32),
            pltpu.VMEM((2, rows, 2 * rows), F32),
            pltpu.VMEM((2, rows, 2 * rows), F32),
            pltpu.VMEM((2 * rows, 2 * rows), BF16),
            pltpu.VMEM((2 * rows, 2 * rows), BF16),
            pltpu.VMEM((rows, BLOCK), BF16),
            pltpu.VMEM((rows, 2 * BLOCK), BF16),
            pltpu.VMEM((rows, 2 * rows), F32),
            pltpu.VMEM((rows, BLOCK), F32),
            pltpu.VMEM((rows, BLOCK), F32),
        ],
        compiler_params=params,
    )(
        conv_input, prior, conv_weight, log_decay, level_weight, grad_out,
        u_act, slope, factors, far_states, grad_end,
    )
    tail_rows, weight_grad = exchange_finish(n, tail, head, wpart, conv_weight)
    grad_input = lax.dynamic_update_slice(grad_input, tail_rows, (rows - 16, 0))
    return (mixed, grad_input, grad_level, weight_grad)


def solution(mesh):
    in_specs = (
        P(("groups", "ctx"), None),
        P(),
        P(None, ("groups", "ctx")),
        P(None, None, ("groups", "ctx")),
        P(("groups", "ctx"), None),
    )
    out_specs = (
        P(("groups", "ctx"), None),
        P(("groups", "ctx"), None),
        P(None, None, ("groups", "ctx")),
        P("groups", None),
    )
    return jax.shard_map(body, mesh=mesh, in_specs=in_specs, out_specs=out_specs, check_vma=False)
```

profile of v0, /device:TPU:0, one launch (start us, length us, event | category | flops | bytes accessed | tf_op | source)
XLA Modules:
  0.0 87.9 jit_solution(5954570464598376462)
XLA Ops:
  0.6 11.2 %shard_map.84 = (bf16[16,2176]{1,0:T(8,128)(2,1)}, f32[16,8,128]{2,1,0:T(8,128)}) custom-call(bf16[128,2176]{1,0:T(8,128)(2,1)} %conv_ref.5, f32[32,128]{1,0:T(8,128)} %decay_ref.5), custom_call_target="tpu_custom_call" | custom-call | tf_op jit(solution)/shard_map/pallas_call | solution.py:103
  11.8 9.4 %shard_map.85 = (bf16[128,2176]{1,0:T(8,128)(2,1)}, f32[128,2176]{1,0:T(8,128)}, f32[2,64,1024]{2,1,0:T(8,128)}, f32[4,2,64,1024]{3,2,1,0:T(8,128)}, f32[2,16,1024]{2,1,0:T(8,128)}) custom-call(bf16[128,2176]{1,0:T(8,128)(2,1)} %conv_ref.5, bf16[16,2176]{1,0:T(8,128)(2,1)} %get-tuple-element.21.prior_ref, f32[4,2176]{1,0:T(4,128)} %w_ref.5, ...), custom_call_target="tpu_custom_call" | custom-call | tf_op jit(solution)/shard_map/pallas_call | solution.py:526
  21.2 31.0 %shard_map.86 = (bf16[4,2,64,1024]{3,2,1,0:T(8,128)(2,1)}, f32[2,64,1024]{2,1,0:T(8,128)}) custom-call(f32[2,64,1024]{2,1,0:T(8,128)} %get-tuple-element.26.end_ref, f32[4,2,64,1024]{3,2,1,0:T(8,128)} %get-tuple-element.27.gf_ref, f32[2,16,1024]{2,1,0:T(8,128)} %get-tuple-element.25.fac_ref), custom_call_target="tpu_custom_call" | custom-call | tf_op jit(solution)/shard_map/pallas_call | solution.py:287
  52.2 15.9 %shard_map.87 = (bf16[128,2048]{1,0:T(8,128)(2,1)}, bf16[128,2176]{1,0:T(8,128)(2,1)}, f32[12,32,128]{2,1,0:T(8,128)}, f32[16,2176]{1,0:T(8,128)}, f32[8,2176]{1,0:T(8,128)}, /*index=5*/f32[8,2176]{1,0:T(8,128)}) custom-call(bf16[128,2176]{1,0:T(8,128)(2,1)} %conv_ref.5, bf16[16,2176]{1,0:T(8,128)(2,1)} %get-tuple-element.21.prior_ref, f32[4,2176]{1,0:T(4,128)} %w_ref.5, ...), custom_call_target="tpu_custom_call" | custom-call | tf_op jit(solution)/shard_map/pallas_call | solution.py:544
  68.1 16.9 %shard_map.88 = (bf16[16,2176]{1,0:T(8,128)(2,1)}, f32[4,2176]{1,0:T(4,128)}) custom-call(f32[16,2176]{1,0:T(8,128)} %get-tuple-element.32.tail_ref, f32[8,2176]{1,0:T(8,128)} %get-tuple-element.33.head_ref, f32[8,2176]{1,0:T(8,128)} %get-tuple-element.34.wpart_ref, f32[4,2176]{1,0:T(4,128)} %w_ref.5), custom_call_target="tpu_custom_call" | custom-call | tf_op jit(solution)/shard_map/pallas_call | solution.py:491
  85.0 1.5 %constant_dynamic-update-slice_fusion = bf16[128,2176]{1,0:T(8,128)(2,1)} fusion(bf16[128,2176]{1,0:T(8,128)(2,1)} %get-tuple-element.31, bf16[16,2176]{1,0:T(8,128)(2,1)} %get-tuple-element.35), kind=kLoop, calls=%fused_computation | loop fusion | bytes 139264 | tf_op jit(solution)/shard_map/dynamic_update_slice | solution.py:578
  86.5 1.4 %copy.11 = f32[4,2176]{1,0:T(4,128)} copy(f32[4,2176]{1,0:T(4,128)} %get-tuple-element.45) | data formatting | bytes 69632
where the time goes:
time: 88.2 us; the launch traced here: 87.9 us
  Pallas kernels  84.3 us (96%)
  local copies, waits for them, and re-layouts  2.9 us (3%)
    pallas_call x1, Pallas kernels, exchange_states(): pl.pallas_call(functools.partial(fenwick_kernel, far), out_shape=(jax.Sha...  31 us
    pallas_call x1, Pallas kernels, exchange_finish(): pl.pallas_call(functools.partial(finish_kernel, n, digits), out_shape=(ja...  16.9 us
    pallas_call x1, Pallas kernels, body(): pl.pallas_call(functools.partial(back_kernel, far), out_shape=(shape((row...  15.9 us
    pallas_call x1, Pallas kernels, exchange_edges(): pl.pallas_call(functools.partial(edge_kernel, n), out_shape=(jax.ShapeDty...  11.2 us
    pallas_call x1, Pallas kernels, body(): pl.pallas_call(functools.partial(front_kernel, far), out_shape=(shape((ro...  9.42 us

commit v1 on v0

--- a/solution.py
+++ b/solution.py
@@ -106,7 +106,7 @@
             jax.ShapeDtypeStruct((16, channels), BF16),
             jax.ShapeDtypeStruct((n, 8, LANES), F32),
         ),
-        in_specs=[vm, vm],
+        in_specs=[pl.BlockSpec(memory_space=pl.ANY), vm],
         out_specs=(vm, vm),
         scratch_shapes=[
             pltpu.VMEM((8, LANES), F32),
@@ -436,18 +436,29 @@
         wpart_ref[:, cols] = jnp.concatenate(sums, axis=0)
 
 
-def finish_kernel(n, digits, tail_ref, head_ref, wpart_ref, w_ref, out_ref, wsum_ref, nxt, acc, slots, hs, hr, send, recv):
+def finish_kernel(n, digits, tail_ref, head_ref, wpart_ref, w_ref, out_ref, wsum_ref, lead, nxt, acc, slots, hs, hr, send, recv):
     me = lax.axis_index("ctx")
     taps = w_ref.shape[0]
+    channels = w_ref.shape[1]
+    width = acc.shape[2]
+    skip = channels - width
+
+    def packed(rows):
+        return jnp.concatenate([rows[:4, :width], rows[:4, skip:]], axis=0)
+
+    def unpacked(value):
+        return jnp.concatenate([value[:4, :skip], value[4:]], axis=1)
+
+    lead[...] = packed(head_ref[...])
+    acc[0] = packed(wpart_ref[...])
     before, after = lax.rem(me + n - 1, n), lax.rem(me + 1, n)
     plan = []
     for shift, size in digits:
         digit = (me >> shift) & (size - 1)
         plan.append((digit, [me ^ (d << shift) for d in range(1, size)]))
     greet([at(before), at(after)] + [at(p) for _, peers in plan for p in peers])
-    row_copy = pltpu.make_async_remote_copy(head_ref, nxt, hs, hr, at(before), MESH)
+    row_copy = pltpu.make_async_remote_copy(lead, nxt, hs, hr, at(before), MESH)
     row_copy.start()
-    acc[0] = wpart_ref[...]
     for stage, (digit, peers) in enumerate(plan):
         copies = []
         for d, peer in enumerate(peers):
@@ -459,9 +470,10 @@
         if stage == 0:
             row_copy.wait()
             keep = jnp.where(me < n - 1, 1.0, 0.0)
-            rows = nxt[...] * keep
-            joined = jnp.concatenate([jnp.zeros((8, rows.shape[1]), F32), rows], axis=0)
-            fix = jnp.zeros((8, rows.shape[1]), F32)
+            rows = unpacked(nxt[...]) * keep
+            blank = jnp.zeros((8, channels), F32)
+            joined = jnp.concatenate([blank, rows, blank[:4]], axis=0)
+            fix = blank
             for k in range(taps - 1):
                 shift = taps - 1 - k
                 fix = fix + w_ref[k : k + 1, :] * joined[shift : shift + 8]
@@ -475,7 +487,7 @@
         else:
             total = (have[0] + have[1]) + (have[2] + have[3])
         acc[stage + 1] = total
-    wsum_ref[...] = acc[len(plan)][:taps]
+    wsum_ref[...] = unpacked(acc[len(plan)])[:taps]
 
 
 def exchange_finish(n, tail, head, wpart, conv_weight):
@@ -487,6 +499,7 @@
         digits.append((shift, 1 << bits))
         shift += bits
     channels = tail.shape[1]
+    width = (channels // LANES + 1) // 2 * LANES
     vm = pl.BlockSpec(memory_space=pltpu.VMEM)
     return pl.pallas_call(
         functools.partial(finish_kernel, n, digits),
@@ -497,9 +510,10 @@
         in_specs=[vm] * 4,
         out_specs=(vm, vm),
         scratch_shapes=[
-            pltpu.VMEM((8, channels), F32),
-            pltpu.VMEM((len(digits) + 1, 8, channels), F32),
-            pltpu.VMEM((len(digits), 3, 8, channels), F32),
+            pltpu.VMEM((8, width), F32),
+            pltpu.VMEM((8, width), F32),
+            pltpu.VMEM((len(digits) + 1, 8, width), F32),
+            pltpu.VMEM((len(digits), 3, 8, width), F32),
             pltpu.SemaphoreType.DMA,
             pltpu.SemaphoreType.DMA,
             pltpu.SemaphoreType.DMA((len(digits), 3)),

time: 88.2 us -> 84.2 us (0.955)
  Pallas kernels: 84.3 us -> 80.3 us
    pallas_call x1, Pallas kernels: 16.9 us -> 12.9 us  [exchange_finish(): pl.pallas_call(functools.partial(finish_kernel, n, digits), out_shape=(ja...]
where the time goes in v1:
time: 84.2 us; the launch traced here: 83.9 us
  Pallas kernels  80.3 us (95%)
  local copies, waits for them, and re-layouts  2.9 us (3%)
    pallas_call x1, Pallas kernels, exchange_states(): pl.pallas_call(functools.partial(fenwick_kernel, far), out_shape=(jax.Sha...  31.1 us
    pallas_call x1, Pallas kernels, body(): pl.pallas_call(functools.partial(back_kernel, far), out_shape=(shape((row...  15.9 us
    pallas_call x1, Pallas kernels, exchange_finish(): pl.pallas_call(functools.partial(finish_kernel, n, digits), out_shape=(ja...  12.9 us
    pallas_call x1, Pallas kernels, exchange_edges(): pl.pallas_call(functools.partial(edge_kernel, n), out_shape=(jax.ShapeDty...  11 us
    pallas_call x1, Pallas kernels, body(): pl.pallas_call(functools.partial(front_kernel, far), out_shape=(shape((ro...  9.42 us

profile of v1, /device:TPU:0, one launch (start us, length us, event | category | flops | bytes accessed | tf_op | source)
XLA Modules:
  0.0 83.9 jit_solution(17830577179197277181)
XLA Ops:
  0.6 11.0 %shard_map.84 = (bf16[16,2176]{1,0:T(8,128)(2,1)}, f32[16,8,128]{2,1,0:T(8,128)}) custom-call(bf16[128,2176]{1,0:T(8,128)(2,1)} %conv_ref.5, f32[32,128]{1,0:T(8,128)} %decay_ref.5), custom_call_target="tpu_custom_call" | custom-call | tf_op jit(solution)/shard_map/pallas_call | solution.py:103
  11.6 9.4 %shard_map.85 = (bf16[128,2176]{1,0:T(8,128)(2,1)}, f32[128,2176]{1,0:T(8,128)}, f32[2,64,1024]{2,1,0:T(8,128)}, f32[4,2,64,1024]{3,2,1,0:T(8,128)}, f32[2,16,1024]{2,1,0:T(8,128)}) custom-call(bf16[128,2176]{1,0:T(8,128)(2,1)} %conv_ref.5, bf16[16,2176]{1,0:T(8,128)(2,1)} %get-tuple-element.21.prior_ref, f32[4,2176]{1,0:T(4,128)} %w_ref.5, ...), custom_call_target="tpu_custom_call" | custom-call | tf_op jit(solution)/shard_map/pallas_call | solution.py:540
  21.0 31.1 %shard_map.86 = (bf16[4,2,64,1024]{3,2,1,0:T(8,128)(2,1)}, f32[2,64,1024]{2,1,0:T(8,128)}) custom-call(f32[2,64,1024]{2,1,0:T(8,128)} %get-tuple-element.26.end_ref, f32[4,2,64,1024]{3,2,1,0:T(8,128)} %get-tuple-element.27.gf_ref, f32[2,16,1024]{2,1,0:T(8,128)} %get-tuple-element.25.fac_ref), custom_call_target="tpu_custom_call" | custom-call | tf_op jit(solution)/shard_map/pallas_call | solution.py:287
  52.1 15.9 %shard_map.87 = (bf16[128,2048]{1,0:T(8,128)(2,1)}, bf16[128,2176]{1,0:T(8,128)(2,1)}, f32[12,32,128]{2,1,0:T(8,128)}, f32[16,2176]{1,0:T(8,128)}, f32[8,2176]{1,0:T(8,128)}, /*index=5*/f32[8,2176]{1,0:T(8,128)}) custom-call(bf16[128,2176]{1,0:T(8,128)(2,1)} %conv_ref.5, bf16[16,2176]{1,0:T(8,128)(2,1)} %get-tuple-element.21.prior_ref, f32[4,2176]{1,0:T(4,128)} %w_ref.5, ...), custom_call_target="tpu_custom_call" | custom-call | tf_op jit(solution)/shard_map/pallas_call | solution.py:558
  68.0 12.9 %shard_map.88 = (bf16[16,2176]{1,0:T(8,128)(2,1)}, f32[4,2176]{1,0:T(4,128)}) custom-call(f32[16,2176]{1,0:T(8,128)} %get-tuple-element.32.tail_ref, f32[8,2176]{1,0:T(8,128)} %get-tuple-element.33.head_ref, f32[8,2176]{1,0:T(8,128)} %get-tuple-element.34.wpart_ref, f32[4,2176]{1,0:T(4,128)} %w_ref.5), custom_call_target="tpu_custom_call" | custom-call | tf_op jit(solution)/shard_map/pallas_call | solution.py:504
  81.0 1.5 %constant_dynamic-update-slice_fusion = bf16[128,2176]{1,0:T(8,128)(2,1)} fusion(bf16[128,2176]{1,0:T(8,128)(2,1)} %get-tuple-element.31, bf16[16,2176]{1,0:T(8,128)(2,1)} %get-tuple-element.35), kind=kLoop, calls=%fused_computation | loop fusion | bytes 139264 | tf_op jit(solution)/shard_map/dynamic_update_slice | solution.py:592
  82.5 1.4 %copy.11 = f32[4,2176]{1,0:T(4,128)} copy(f32[4,2176]{1,0:T(4,128)} %get-tuple-element.45) | data formatting | bytes 69632

commit v2 on v1

--- a/solution.py
+++ b/solution.py
@@ -205,8 +205,72 @@
             gf_ref[level, side, :, out] = dot(q_t, jnp.concatenate(split2(inner), axis=0))
 
 
+def near_setup(decay_ref, lw_ref, u_ref, glev_ref, facs, cum3, cum_rows, bias, scores, hotx, hotg, ds_acc):
+    rows = decay_ref.shape[1]
+    wide = 2 * rows
+    cum = running_decay(decay_ref)
+    cum_rows[...] = cum.T
+    cum3[...] = jnp.concatenate(split3(cum), axis=1)
+    for level in range(2):
+        value = lw_ref[level].T * level_scale(level)
+        facs[level * rows : (level + 1) * rows, :] = jnp.concatenate(split2(value), axis=1)
+    first = iota((rows, wide), 0)
+    second = iota((rows, wide), 1) % rows
+    bias[0] = jnp.where(second <= first, 0.0, -1e30)
+    bias[1] = jnp.where(first <= second, 0.0, -1e30)
+    r, c = iota((wide, wide), 0), iota((wide, wide), 1)
+    same = (r // rows) == (c % LANES) // BLOCK
+    block1 = (r % rows) // BLOCK == 1
+    hotg[...] = jnp.where(same, 1.0, 0.0).astype(BF16)
+    hotx[...] = jnp.where(same & (block1 == (c < LANES)), 1.0, 0.0).astype(BF16)
+    bq = u_ref[:, u_ref.shape[1] - LANES :]
+    b, q = bq[:, :BLOCK], bq[:, BLOCK:]
+    scores[0] = dot_nt(q, jnp.concatenate([b, b], axis=0))
+    scores[1] = dot_nt(b, jnp.concatenate([q, q], axis=0))
+    ds_acc[...] = jnp.zeros_like(ds_acc)
+    glev_ref[...] = jnp.zeros_like(glev_ref)
+
+
+def head_pick(heads, j):
+    lanes = iota((heads, 2 * LANES), 1) % LANES
+    return jnp.where(iota((heads, 2 * LANES), 0) == 2 * j + lanes // BLOCK, 1.0, 0.0).astype(BF16)
+
+
+def near_pair(j, g_ref, u_ref, mixed_ref, dx_ref, glev_ref, facs, cum3, cum_rows, bias, scores, hotx, hotg, ds_acc):
+    heads, rows = cum_rows.shape
+    wide = 2 * rows
+    low = iota((rows, LANES), 0) < BLOCK
+    cols = pl.ds(pl.multiple_of(j * LANES, LANES), LANES)
+    x = u_ref[:, cols]
+    g = g_ref[:, cols].astype(F32)
+    spread = dot(facs[...], one_hot(2 * heads, heads, 2 * j, LANES, BLOCK))
+    w0, w1 = spread[:rows], spread[rows:]
+    col = dot(cum3[...], one_hot(3 * heads, heads, 2 * j, wide, rows))
+    row = jnp.concatenate([cum_rows[pl.ds(2 * j, 1), :], cum_rows[pl.ds(2 * j + 1, 1), :]], axis=1)
+    gap = col - row
+    decay = jnp.exp(gap + bias[0])
+    mix = (scores[0] * decay).astype(BF16)
+    mix_t = (scores[1] * jnp.exp(bias[1] - gap)).astype(BF16)
+    wx = jnp.concatenate([jnp.concatenate([x, x], axis=1)] * 2, axis=0) * hotx[...]
+    res = dot(mix, wx)
+    out0 = jnp.where(low, res[:, LANES:], res[:, :LANES])
+    out1 = jnp.where(low, 0.0, res[:, LANES:])
+    gz = (g * w0).astype(BF16)
+    gh = (g * jnp.where(low, w0, w1)).astype(BF16)
+    gg = jnp.concatenate([gz, gh], axis=1)
+    ds_acc[...] += decay * dot_nt(gg, wx)
+    res = dot(mix_t, jnp.concatenate([gg, gg], axis=0) * hotg[...])
+    dx_ref[:, cols] = jnp.where(low, res[:, LANES:], res[:, :LANES])
+    mixed_ref[:, cols] = w0 * out0 + w1 * out1
+    pick = head_pick(heads, j)
+    for level, out in enumerate((out0, out1)):
+        glev_ref[level] += dot_nt(pick, jnp.concatenate(split2(g * out), axis=1)) * level_scale(level)
+
+
 def fenwick_kernel(
-    far, end_ref, gf_ref, fac_ref, far_ref, grad_ref,
+    far, end_ref, gf_ref, fac_ref, decay_ref, lw_ref, g_ref, u_ref,
+    far_ref, grad_ref, mixed_ref, dx_ref, glev_ref, dbq_ref,
+    facs, cum3, cum_rows, bias, scores, hotx, hotg, ds_acc,
     up0, up0_in, up, up_in, cross_in, merge, merge_in, down, down_in, last, last_in,
     sems_s, sems_r, run, back,
 ):
@@ -237,6 +301,18 @@
     def sib_coef(level):
         return fac_ref[core, 2 * level + 1 : 2 * level + 2, :]
 
+    near_setup(decay_ref, lw_ref, u_ref, glev_ref, facs, cum3, cum_rows, bias, scores, hotx, hotg, ds_acc)
+    pairs = g_ref.shape[1] // LANES
+    cuts = [0, 1] + [1 + (pairs - 1) * (step + 1) // (far - 1) for step in range(far - 1)]
+
+    def near_part(lo, hi):
+        @pl.loop(lo, hi)
+        def _(j):
+            near_pair(
+                j, g_ref, u_ref, mixed_ref, dx_ref, glev_ref, facs, cum3, cum_rows, bias, scores, hotx, hotg, ds_acc
+            )
+
+    near_part(cuts[0], cuts[1])
     merge_copy.wait()
     pending_down = None
     for step in range(far - 1):
@@ -258,6 +334,7 @@
             run[...] = run[...] * own_coef(step) + up_in[step - 1].astype(F32) * sib_coef(step)
         up[step] = run[...].astype(BF16)
         up_copy = copy(up.at[step], up_in.at[step], 1, step + 1, peers[step + 1])
+        near_part(cuts[step + 1], cuts[step + 2])
     pending_down.wait()
     if far > 2:
         back[...] = back[...] * own_coef(1) + down_in[0].astype(F32)
@@ -266,6 +343,12 @@
     last[core] = (gf_ref[0, core] + back[...] * sib_coef(0)).astype(BF16)
     last[other] = gf_ref[0, other].astype(BF16)
     last_copy = copy(last, last_in, 4, 0, peers[0])
+    rows = decay_ref.shape[1]
+    bq = u_ref[:, u_ref.shape[1] - LANES :]
+    ds = ds_acc[:, :rows] + ds_acc[:, rows:]
+    dq = dot(ds.astype(BF16), bq[:, :BLOCK])
+    db = dot(ds.T.astype(BF16), bq[:, BLOCK:])
+    dbq_ref[...] = jnp.concatenate([db, dq], axis=1)
     up_copy.wait()
     crosses.append(copy(up_in.at[far - 2], cross_in.at[far - 2], 3, far - 1, peers[0]))
     far_ref[0] = up0_in[...]
@@ -279,20 +362,34 @@
         far_ref[level, other] = cross_in[level - 1]
 
 
-def exchange_states(far, end_state, grad_far, factors):
+def exchange_states(far, end_state, grad_far, factors, log_decay, level_weight, grad_out, u_act):
     half = end_state.shape
     piece = half[1:]
     vm = pl.BlockSpec(memory_space=pltpu.VMEM)
     stack = (far - 1,) + piece
+    heads, rows = log_decay.shape
+    channels = grad_out.shape[1]
     return pl.pallas_call(
         functools.partial(fenwick_kernel, far),
         out_shape=(
             jax.ShapeDtypeStruct((far,) + half, BF16),
             jax.ShapeDtypeStruct(half, F32),
-        ),
-        in_specs=[vm] * 3,
-        out_specs=(vm, vm),
+            jax.ShapeDtypeStruct((rows, channels), F32),
+            jax.ShapeDtypeStruct((rows, channels), F32),
+            jax.ShapeDtypeStruct((2, heads, rows), F32),
+            jax.ShapeDtypeStruct((rows, LANES), F32),
+        ),
+        in_specs=[vm] * 7,
+        out_specs=(vm,) * 6,
         scratch_shapes=[
+            pltpu.VMEM((2 * rows, 2 * heads), BF16),
+            pltpu.VMEM((rows, 3 * heads), BF16),
+            pltpu.VMEM((heads, rows), F32),
+            pltpu.VMEM((2, rows, 2 * rows), F32),
+            pltpu.VMEM((2, rows, 2 * rows), F32),
+            pltpu.VMEM((2 * rows, 2 * rows), BF16),
+            pltpu.VMEM((2 * rows, 2 * rows), BF16),
+            pltpu.VMEM((rows, 2 * rows), F32),
             pltpu.VMEM(half, BF16),
             pltpu.VMEM(half, BF16),
             pltpu.VMEM(stack, BF16),
@@ -312,48 +409,32 @@
         compiler_params=pltpu.CompilerParams(
             collective_id=1, has_side_effects=True, vmem_limit_bytes=VMEM_LIMIT
         ),
-    )(end_state, grad_far, factors)
+    )(end_state, grad_far, factors, log_decay, level_weight, grad_out, u_act)
 
 
 def back_kernel(
     far, conv_ref, prior_ref, w_ref, decay_ref, lw_ref, g_ref, u_ref, slope_ref, fac_ref, far_ref, grad_ref,
+    near_ref, dx_ref, nlev_ref, dbq_ref,
     mixed_ref, gin_ref, glev_ref, tail_ref, head_ref, wpart_ref,
-    pad, gp, facs, cum3, cum_rows, bias, scores, hotx, hotg, q_s, b2_s, ds_acc, dq_acc, db_acc,
+    pad, gp, facs, q_s, b2_s, dq_acc, db_acc,
 ):
     rows, channels = g_ref.shape
     heads = decay_ref.shape[0]
     taps = w_ref.shape[0]
-    wide = 2 * rows
     fill_padded(pad, conv_ref, prior_ref)
     cum = running_decay(decay_ref)
-    cum_rows[...] = cum.T
-    cum3[...] = jnp.concatenate(split3(cum), axis=1)
-    base = [lw_ref[0].T * level_scale(0), lw_ref[1].T * level_scale(1)]
-    base += [jnp.exp(cum[rows - 1 : rows] - cum), jnp.exp(cum)]
+    base = [jnp.exp(cum[rows - 1 : rows] - cum), jnp.exp(cum)]
     base += [lw_ref[2 + level].T * level_scale(2 + level) for level in range(far)]
     for idx, value in enumerate(base):
         facs[idx * rows : (idx + 1) * rows, :] = jnp.concatenate(split2(value), axis=1)
-    first = iota((rows, wide), 0)
-    second = iota((rows, wide), 1) % rows
-    bias[0] = jnp.where(second <= first, 0.0, -1e30)
-    bias[1] = jnp.where(first <= second, 0.0, -1e30)
-    r, c = iota((wide, wide), 0), iota((wide, wide), 1)
-    same = (r // rows) == (c % LANES) // BLOCK
-    block1 = (r % rows) // BLOCK == 1
-    hotg[...] = jnp.where(same, 1.0, 0.0).astype(BF16)
-    hotx[...] = jnp.where(same & (block1 == (c < LANES)), 1.0, 0.0).astype(BF16)
     bq = u_ref[:, channels:]
-    b, q = bq[:, :BLOCK], bq[:, BLOCK:]
-    q_s[...] = q
-    b2_s[...] = jnp.concatenate([b, b], axis=1)
-    scores[0] = dot_nt(q, jnp.concatenate([b, b], axis=0))
-    scores[1] = dot_nt(b, jnp.concatenate([q, q], axis=0))
-    ds_acc[...] = jnp.zeros_like(ds_acc)
+    q_s[...] = bq[:, BLOCK:]
+    b2_s[...] = jnp.concatenate([bq[:, :BLOCK]] * 2, axis=1)
     dq_acc[...] = jnp.zeros_like(dq_acc)
     db_acc[...] = jnp.zeros_like(db_acc)
     glev_ref[...] = jnp.zeros_like(glev_ref)
+    glev_ref[0:2] = nlev_ref[...]
     per_half = channels // 2 // LANES
-    low = iota((rows, LANES), 0) < BLOCK
 
     @pl.loop(0, channels // LANES)
     def _(j):
@@ -367,55 +448,33 @@
         def fac(idx):
             return spread[idx * rows : (idx + 1) * rows]
 
-        w0, w1 = fac(0), fac(1)
-        col = dot(cum3[...], one_hot(3 * heads, heads, 2 * j, wide, rows))
-        row = jnp.concatenate([cum_rows[pl.ds(2 * j, 1), :], cum_rows[pl.ds(2 * j + 1, 1), :]], axis=1)
-        gap = col - row
-        decay = jnp.exp(gap + bias[0])
-        mix = (scores[0] * decay).astype(BF16)
-        mix_t = (scores[1] * jnp.exp(bias[1] - gap)).astype(BF16)
-        wx = jnp.concatenate([jnp.concatenate([x, x], axis=1)] * 2, axis=0) * hotx[...]
-        res = dot(mix, wx)
-        out0 = jnp.where(low, res[:, LANES:], res[:, :LANES])
-        out1 = jnp.where(low, 0.0, res[:, LANES:])
-        gz = (g * w0).astype(BF16)
-        gh = (g * jnp.where(low, w0, w1)).astype(BF16)
-        gg = jnp.concatenate([gz, gh], axis=1)
-        ds_acc[...] += decay * dot_nt(gg, wx)
-        res = dot(mix_t, jnp.concatenate([gg, gg], axis=0) * hotg[...])
-        dx = jnp.where(low, res[:, LANES:], res[:, :LANES])
-
-        mixed = w0 * out0 + w1 * out1
-        products = [g * out0, g * out1]
-        inner, states = [], []
+        mixed = near_ref[:, cols]
+        products, inner, states = [], [], []
         for level in range(far):
             state = far_ref[level, side, :, part]
-            scale = fac(3) * fac_ref[side, 2 * far + level : 2 * far + level + 1, part]
+            scale = fac(1) * fac_ref[side, 2 * far + level : 2 * far + level + 1, part]
             out = dot(q_s[...], state) * scale
-            weight = fac(4 + level)
+            weight = fac(2 + level)
             mixed = mixed + weight * out
             products.append(g * out)
             inner.append((g * weight * scale).astype(BF16))
             states.append(state)
         mixed_ref[:, cols] = mixed.astype(BF16)
         dq_acc[...] += dot_nt(jnp.concatenate(inner, axis=1), jnp.concatenate(states, axis=1))
-        pick = jnp.where(
-            iota((heads, 2 * LANES), 0) == 2 * j + (iota((heads, 2 * LANES), 1) % LANES) // BLOCK, 1.0, 0.0
-        ).astype(BF16)
+        pick = head_pick(heads, j)
         for level, product in enumerate(products):
-            glev_ref[level] += dot_nt(pick, jnp.concatenate(split2(product), axis=1)) * level_scale(level)
+            sums = dot_nt(pick, jnp.concatenate(split2(product), axis=1))
+            glev_ref[2 + level] += sums * level_scale(2 + level)
 
         grad = grad_ref[side, :, part]
         hi, lo = split2(grad)
-        key_decay = fac(2)
-        dx = dx + key_decay * dot(b2_s[...], jnp.concatenate([hi, lo], axis=0))
+        key_decay = fac(0)
+        dx = dx_ref[:, cols] + key_decay * dot(b2_s[...], jnp.concatenate([hi, lo], axis=0))
         db_acc[...] += dot_nt((x.astype(F32) * key_decay).astype(BF16), hi)
         gp[0:rows, cols] = dx * slope_ref[:, cols]
 
-    ds = ds_acc[:, :rows] + ds_acc[:, rows:]
-    dq = dq_acc[...] + dot(ds.astype(BF16), b)
-    db = db_acc[...] + dot(ds.T.astype(BF16), q)
-    gp[0:rows, channels:] = jnp.concatenate([db, dq], axis=1) * slope_ref[:, channels:]
+    dbq = dbq_ref[...] + jnp.concatenate([db_acc[...], dq_acc[...]], axis=1)
+    gp[0:rows, channels:] = dbq * slope_ref[:, channels:]
     gp[rows:, :] = jnp.zeros((8, gp.shape[1]), F32)
     head_ref[...] = gp[0:8, :]
 
@@ -554,7 +613,9 @@
         ],
         compiler_params=params,
     )(conv_input, prior, conv_weight, log_decay, level_weight, grad_out, totals)
-    far_states, grad_end = exchange_states(far, end_state, grad_far, factors)
+    far_states, grad_end, *near = exchange_states(
+        far, end_state, grad_far, factors, log_decay, level_weight, grad_out, u_act
+    )
     mixed, grad_input, grad_level, tail, head, wpart = pl.pallas_call(
         functools.partial(back_kernel, far),
         out_shape=(
@@ -565,28 +626,21 @@
             shape((8, conv_ch), F32),
             shape((8, conv_ch), F32),
         ),
-        in_specs=[vm] * 11,
+        in_specs=[vm] * 15,
         out_specs=(vm,) * 6,
         scratch_shapes=[
             pltpu.VMEM((rows + 8, conv_ch), F32),
             pltpu.VMEM((rows + 8, conv_ch), F32),
-            pltpu.VMEM(((4 + far) * rows, 2 * heads), BF16),
-            pltpu.VMEM((rows, 3 * heads), BF16),
-            pltpu.VMEM((heads, rows), F32),
-            pltpu.VMEM((2, rows, 2 * rows), F32),
-            pltpu.VMEM((2, rows, 2 * rows), F32),
-            pltpu.VMEM((2 * rows, 2 * rows), BF16),
-            pltpu.VMEM((2 * rows, 2 * rows), BF16),
+            pltpu.VMEM(((2 + far) * rows, 2 * heads), BF16),
             pltpu.VMEM((rows, BLOCK), BF16),
             pltpu.VMEM((rows, 2 * BLOCK), BF16),
-            pltpu.VMEM((rows, 2 * rows), F32),
             pltpu.VMEM((rows, BLOCK), F32),
             pltpu.VMEM((rows, BLOCK), F32),
         ],
         compiler_params=params,
     )(
         conv_input, prior, conv_weight, log_decay, level_weight, grad_out,
-        u_act, slope, factors, far_states, grad_end,
+        u_act, slope, factors, far_states, grad_end, *near,
     )
     tail_rows, weight_grad = exchange_finish(n, tail, head, wpart, conv_weight)
     grad_input = lax.dynamic_update_slice(grad_input, tail_rows, (rows - 16, 0))

time: 84.2 us -> 82.8 us (0.983)
  Pallas kernels: 80.3 us -> 79 us
    pallas_call x1, Pallas kernels: 15.9 us -> 13.4 us  [body(): pl.pallas_call(functools.partial(back_kernel, far), out_shape=(shape((row...]
    pallas_call x1, Pallas kernels: 31.1 us -> 32.2 us  [exchange_states(): pl.pallas_call(functools.partial(fenwick_kernel, far), out_shape=(jax.Sha...]
where the time goes in v2:
time: 82.8 us; the launch traced here: 82.5 us
  Pallas kernels  79 us (95%)
  local copies, waits for them, and re-layouts  2.9 us (4%)
    pallas_call x1, Pallas kernels, exchange_states(): pl.pallas_call(functools.partial(fenwick_kernel, far), out_shape=(jax.Sha...  32.2 us
    pallas_call x1, Pallas kernels, body(): pl.pallas_call(functools.partial(back_kernel, far), out_shape=(shape((row...  13.4 us
    pallas_call x1, Pallas kernels, exchange_finish(): pl.pallas_call(functools.partial(finish_kernel, n, digits), out_shape=(ja...  12.9 us
    pallas_call x1, Pallas kernels, exchange_edges(): pl.pallas_call(functools.partial(edge_kernel, n), out_shape=(jax.ShapeDty...  11 us
    pallas_call x1, Pallas kernels, body(): pl.pallas_call(functools.partial(front_kernel, far), out_shape=(shape((ro...  9.43 us

profile of v2, /device:TPU:0, one launch (start us, length us, event | category | flops | bytes accessed | tf_op | source)
XLA Modules:
  0.0 82.5 jit_solution(2420050835295116640)
XLA Ops:
  0.6 11.0 %shard_map.84 = (bf16[16,2176]{1,0:T(8,128)(2,1)}, f32[16,8,128]{2,1,0:T(8,128)}) custom-call(bf16[128,2176]{1,0:T(8,128)(2,1)} %conv_ref.5, f32[32,128]{1,0:T(8,128)} %decay_ref.7), custom_call_target="tpu_custom_call" | custom-call | tf_op jit(solution)/shard_map/pallas_call | solution.py:103
  11.6 9.4 %shard_map.85 = (bf16[128,2176]{1,0:T(8,128)(2,1)}, f32[128,2176]{1,0:T(8,128)}, f32[2,64,1024]{2,1,0:T(8,128)}, f32[4,2,64,1024]{3,2,1,0:T(8,128)}, f32[2,16,1024]{2,1,0:T(8,128)}) custom-call(bf16[128,2176]{1,0:T(8,128)(2,1)} %conv_ref.5, bf16[16,2176]{1,0:T(8,128)(2,1)} %get-tuple-element.25.prior_ref, f32[4,2176]{1,0:T(4,128)} %w_ref.5, ...), custom_call_target="tpu_custom_call" | custom-call | tf_op jit(solution)/shard_map/pallas_call | solution.py:599
  21.0 32.2 %shard_map.86 = (bf16[4,2,64,1024]{3,2,1,0:T(8,128)(2,1)}, f32[2,64,1024]{2,1,0:T(8,128)}, f32[128,2048]{1,0:T(8,128)}, f32[128,2048]{1,0:T(8,128)}, f32[2,32,128]{2,1,0:T(8,128)}, /*index=5*/f32[128,128]{1,0:T(8,128)}) custom-call(f32[2,64,1024]{2,1,0:T(8,128)} %get-tuple-element.30.end_ref, f32[4,2,64,1024]{3,2,1,0:T(8,128)} %get-tuple-element.31.gf_ref, ...), custom_call_target="tpu_custom_call" | custom-call | tf_op jit(solution)/shard_map/pallas_call | solution.py:372
  53.3 13.4 %shard_map.87 = (bf16[128,2048]{1,0:T(8,128)(2,1)}, bf16[128,2176]{1,0:T(8,128)(2,1)}, f32[12,32,128]{2,1,0:T(8,128)}, f32[16,2176]{1,0:T(8,128)}, f32[8,2176]{1,0:T(8,128)}, /*index=5*/f32[8,2176]{1,0:T(8,128)}) custom-call(bf16[128,2176]{1,0:T(8,128)(2,1)} %conv_ref.5, bf16[16,2176]{1,0:T(8,128)(2,1)} %get-tuple-element.25.prior_ref, f32[4,2176]{1,0:T(4,128)} %w_ref.5, ...), custom_call_target="tpu_custom_call" | custom-call | tf_op jit(solution)/shard_map/pallas_call | solution.py:619
  66.7 12.9 %shard_map.88 = (bf16[16,2176]{1,0:T(8,128)(2,1)}, f32[4,2176]{1,0:T(4,128)}) custom-call(f32[16,2176]{1,0:T(8,128)} %get-tuple-element.40.tail_ref, f32[8,2176]{1,0:T(8,128)} %get-tuple-element.41.head_ref, f32[8,2176]{1,0:T(8,128)} %get-tuple-element.42.wpart_ref, f32[4,2176]{1,0:T(4,128)} %w_ref.5), custom_call_target="tpu_custom_call" | custom-call | tf_op jit(solution)/shard_map/pallas_call | solution.py:563
  79.6 1.5 %constant_dynamic-update-slice_fusion = bf16[128,2176]{1,0:T(8,128)(2,1)} fusion(bf16[128,2176]{1,0:T(8,128)(2,1)} %get-tuple-element.39, bf16[16,2176]{1,0:T(8,128)(2,1)} %get-tuple-element.43), kind=kLoop, calls=%fused_computation | loop fusion | bytes 139264 | tf_op jit(solution)/shard_map/dynamic_update_slice | solution.py:646
  81.1 1.4 %copy.11 = f32[4,2176]{1,0:T(4,128)} copy(f32[4,2176]{1,0:T(4,128)} %get-tuple-element.53) | data formatting | bytes 69632

commit v3 on v2

--- a/solution.py
+++ b/solution.py
@@ -63,7 +63,7 @@
     return (lax.axis_index("groups"), peer)
 
 
-def edge_kernel(n, conv_ref, decay_ref, prior_ref, totals_ref, mine, slots, rows, send, recv, rsend, rrecv):
+def start_edges(n, conv_ref, decay_ref, prior_ref, totals_ref, mine, slots, rows, send, recv, rsend, rrecv):
     me = lax.axis_index("ctx")
     peers = [lax.rem(me + d, n) for d in range(1, n)]
     heads = decay_ref.shape[0]
@@ -89,38 +89,16 @@
         copy.start()
         copies.append(copy)
     totals_ref[me] = mine[...]
-    for d in range(1, n):
-        copies[d - 1].wait()
-        totals_ref[lax.rem(me - d + n, n)] = slots[d - 1]
-    row_copy.wait()
-    keep = jnp.where(me > 0, 1.0, 0.0)
-    prior_ref[...] = (rows[...].astype(F32) * keep).astype(BF16)
-
-
-def exchange_edges(n, conv_input, log_decay):
-    channels = conv_input.shape[1]
-    vm = pl.BlockSpec(memory_space=pltpu.VMEM)
-    return pl.pallas_call(
-        functools.partial(edge_kernel, n),
-        out_shape=(
-            jax.ShapeDtypeStruct((16, channels), BF16),
-            jax.ShapeDtypeStruct((n, 8, LANES), F32),
-        ),
-        in_specs=[pl.BlockSpec(memory_space=pl.ANY), vm],
-        out_specs=(vm, vm),
-        scratch_shapes=[
-            pltpu.VMEM((8, LANES), F32),
-            pltpu.VMEM((n - 1, 8, LANES), F32),
-            pltpu.VMEM((16, channels), BF16),
-            pltpu.SemaphoreType.DMA((n - 1,)),
-            pltpu.SemaphoreType.DMA((n - 1,)),
-            pltpu.SemaphoreType.DMA,
-            pltpu.SemaphoreType.DMA,
-        ],
-        compiler_params=pltpu.CompilerParams(
-            collective_id=0, has_side_effects=True, vmem_limit_bytes=VMEM_LIMIT
-        ),
-    )(conv_input, log_decay)
+
+    def finish():
+        for d in range(1, n):
+            copies[d - 1].wait()
+            totals_ref[lax.rem(me - d + n, n)] = slots[d - 1]
+        row_copy.wait()
+        keep = jnp.where(me > 0, 1.0, 0.0)
+        prior_ref[...] = (rows[...].astype(F32) * keep).astype(BF16)
+
+    return finish
 
 
 def fill_padded(pad, conv_ref, prior_ref):
@@ -135,15 +113,38 @@
     return by_token
 
 
-def front_kernel(
-    far, conv_ref, prior_ref, w_ref, decay_ref, lw_ref, g_ref, totals_ref,
+def front_part(
+    far, finish_edges, conv_ref, prior_ref, w_ref, decay_ref, lw_ref, g_ref, totals_ref,
     u_ref, slope_ref, end_ref, gf_ref, fac_ref, pad, facs,
 ):
     me = lax.axis_index("ctx")
     rows, channels = g_ref.shape
     heads = decay_ref.shape[0]
     taps = w_ref.shape[0]
-    fill_padded(pad, conv_ref, prior_ref)
+    pad[0:8, :] = jnp.zeros((8, pad.shape[1]), F32)
+    pad[8:, :] = conv_ref[...].astype(F32)
+
+    def activate(cols, count):
+        top = 8 - taps + 1
+        acc = w_ref[0:1, cols] * pad[top : top + count, cols]
+        for k in range(1, taps):
+            acc = acc + w_ref[k : k + 1, cols] * pad[top + k : top + k + count, cols]
+        sig = jax.nn.sigmoid(acc)
+        u_ref[0:count, cols] = (acc * sig).astype(BF16)
+        slope_ref[0:count, cols] = sig * (1.0 + acc * (1.0 - sig))
+
+    @pl.loop(0, pad.shape[1] // LANES)
+    def _(j):
+        activate(pl.ds(pl.multiple_of(j * LANES, LANES), LANES), rows)
+
+    cum = running_decay(decay_ref)
+    finish_edges()
+    pad[0:8, :] = prior_ref[...].astype(F32)[8:16]
+
+    @pl.loop(0, pad.shape[1] // LANES)
+    def _(j):
+        activate(pl.ds(pl.multiple_of(j * LANES, LANES), LANES), 16)
+
     totals = totals_ref[...][:, 0, :heads]
     spans = iota(totals.shape, 0)
 
@@ -166,7 +167,6 @@
         stack.append(jnp.zeros((count - len(stack), heads), F32))
     small = jnp.concatenate(split2(jnp.concatenate(stack, axis=0)), axis=1)
 
-    cum = running_decay(decay_ref)
     in_device = jnp.exp(cum)
     base = [jnp.exp(cum[rows - 1 : rows] - cum)]
     for level in range(far):
@@ -174,17 +174,7 @@
     for idx, value in enumerate(base):
         facs[idx * rows : (idx + 1) * rows, :] = jnp.concatenate(split2(value), axis=1)
 
-    def activate(cols):
-        acc = w_ref[0:1, cols] * pad[8 - taps + 1 : 8 - taps + 1 + rows, cols]
-        for k in range(1, taps):
-            acc = acc + w_ref[k : k + 1, cols] * pad[8 - taps + 1 + k : 8 - taps + 1 + k + rows, cols]
-        sig = jax.nn.sigmoid(acc)
-        u = (acc * sig).astype(BF16)
-        u_ref[:, cols] = u
-        slope_ref[:, cols] = sig * (1.0 + acc * (1.0 - sig))
-        return u
-
-    bq = activate(pl.ds(channels, LANES)).astype(F32).T.astype(BF16)
+    bq = u_ref[:, channels:].astype(F32).T.astype(BF16)
     b_t = jnp.concatenate([bq[:BLOCK]] * 2, axis=1)
     q_t = jnp.concatenate([bq[BLOCK:]] * 2, axis=1)
     per_half = channels // 2 // LANES
@@ -194,7 +184,7 @@
         cols = pl.ds(pl.multiple_of(j * LANES, LANES), LANES)
         side = j // per_half
         out = pl.ds(pl.multiple_of((j % per_half) * LANES, LANES), LANES)
-        x = activate(cols).astype(F32)
+        x = u_ref[:, cols].astype(F32)
         hot = one_hot(2 * heads, heads, 2 * j, LANES, BLOCK)
         spread = dot(facs[...], hot)
         fac_ref[side, :, out] = dot(small, hot)
@@ -267,7 +257,7 @@
         glev_ref[level] += dot_nt(pick, jnp.concatenate(split2(g * out), axis=1)) * level_scale(level)
 
 
-def fenwick_kernel(
+def fenwick_part(
     far, end_ref, gf_ref, fac_ref, decay_ref, lw_ref, g_ref, u_ref,
     far_ref, grad_ref, mixed_ref, dx_ref, glev_ref, dbq_ref,
     facs, cum3, cum_rows, bias, scores, hotx, hotg, ds_acc,
@@ -290,7 +280,6 @@
     up0[...] = end_ref[...].astype(BF16)
     for level in range(1, far):
         merge[level - 1] = gf_ref[level, other].astype(BF16)
-    greet(peers)
     merge_copy = copy(merge, merge_in, 0, 0, peers[0])
     up_copy = copy(up0, up0_in, 1, 0, peers[0])
     crosses = []
@@ -362,26 +351,62 @@
         far_ref[level, other] = cross_in[level - 1]
 
 
-def exchange_states(far, end_state, grad_far, factors, log_decay, level_weight, grad_out, u_act):
-    half = end_state.shape
-    piece = half[1:]
-    vm = pl.BlockSpec(memory_space=pltpu.VMEM)
-    stack = (far - 1,) + piece
+def travel_kernel(
+    n, far, conv_ref, w_ref, decay_ref, lw_ref, g_ref,
+    prior_ref, u_ref, slope_ref, fac_ref, far_ref, grad_ref, mixed_ref, dx_ref, glev_ref, dbq_ref,
+    totals, mine, slots, rows, send, recv, rsend, rrecv, pad, facs, end, gf, *rest,
+):
+    finish = start_edges(n, conv_ref, decay_ref, prior_ref, totals, mine, slots, rows, send, recv, rsend, rrecv)
+    front_part(
+        far, finish, conv_ref, prior_ref, w_ref, decay_ref, lw_ref, g_ref, totals,
+        u_ref, slope_ref, end, gf, fac_ref, pad, facs,
+    )
+    fenwick_part(
+        far, end, gf, fac_ref, decay_ref, lw_ref, g_ref, u_ref,
+        far_ref, grad_ref, mixed_ref, dx_ref, glev_ref, dbq_ref, *rest,
+    )
+
+
+def travel(n, conv_input, conv_weight, log_decay, level_weight, grad_out):
+    far = n.bit_length() - 1
     heads, rows = log_decay.shape
     channels = grad_out.shape[1]
+    conv_ch = conv_input.shape[1]
+    piece = (BLOCK, channels // 2)
+    half = (2,) + piece
+    stack = (far - 1,) + piece
+    fac_rows = (3 * far + 7) // 8 * 8
+    shape = jax.ShapeDtypeStruct
+    vm = pl.BlockSpec(memory_space=pltpu.VMEM)
     return pl.pallas_call(
-        functools.partial(fenwick_kernel, far),
+        functools.partial(travel_kernel, n, far),
         out_shape=(
-            jax.ShapeDtypeStruct((far,) + half, BF16),
-            jax.ShapeDtypeStruct(half, F32),
-            jax.ShapeDtypeStruct((rows, channels), F32),
-            jax.ShapeDtypeStruct((rows, channels), F32),
-            jax.ShapeDtypeStruct((2, heads, rows), F32),
-            jax.ShapeDtypeStruct((rows, LANES), F32),
+            shape((16, conv_ch), BF16),
+            shape((rows, conv_ch), BF16),
+            shape((rows, conv_ch), F32),
+            shape((2, fac_rows, channels // 2), F32),
+            shape((far,) + half, BF16),
+            shape(half, F32),
+            shape((rows, channels), F32),
+            shape((rows, channels), F32),
+            shape((2, heads, rows), F32),
+            shape((rows, LANES), F32),
         ),
-        in_specs=[vm] * 7,
-        out_specs=(vm,) * 6,
+        in_specs=[vm] * 5,
+        out_specs=(vm,) * 10,
         scratch_shapes=[
+            pltpu.VMEM((n, 8, LANES), F32),
+            pltpu.VMEM((8, LANES), F32),
+            pltpu.VMEM((n - 1, 8, LANES), F32),
+            pltpu.VMEM((16, conv_ch), BF16),
+            pltpu.SemaphoreType.DMA((n - 1,)),
+            pltpu.SemaphoreType.DMA((n - 1,)),
+            pltpu.SemaphoreType.DMA,
+            pltpu.SemaphoreType.DMA,
+            pltpu.VMEM((rows + 8, conv_ch), F32),
+            pltpu.VMEM(((1 + far) * rows, 2 * heads), BF16),
+            pltpu.VMEM(half, F32),
+            pltpu.VMEM((far,) + half, F32),
             pltpu.VMEM((2 * rows, 2 * heads), BF16),
             pltpu.VMEM((rows, 3 * heads), BF16),
             pltpu.VMEM((heads, rows), F32),
@@ -392,13 +417,7 @@
             pltpu.VMEM((rows, 2 * rows), F32),
             pltpu.VMEM(half, BF16),
             pltpu.VMEM(half, BF16),
-            pltpu.VMEM(stack, BF16),
-            pltpu.VMEM(stack, BF16),
-            pltpu.VMEM(stack, BF16),
-            pltpu.VMEM(stack, BF16),
-            pltpu.VMEM(stack, BF16),
-            pltpu.VMEM(stack, BF16),
-            pltpu.VMEM(stack, BF16),
+            *[pltpu.VMEM(stack, BF16)] * 7,
             pltpu.VMEM(half, BF16),
             pltpu.VMEM(half, BF16),
             pltpu.SemaphoreType.DMA((5, far)),
@@ -407,9 +426,9 @@
             pltpu.VMEM(piece, F32),
         ],
         compiler_params=pltpu.CompilerParams(
-            collective_id=1, has_side_effects=True, vmem_limit_bytes=VMEM_LIMIT
+            collective_id=0, has_side_effects=True, vmem_limit_bytes=VMEM_LIMIT
         ),
-    )(end_state, grad_far, factors, log_decay, level_weight, grad_out, u_act)
+    )(conv_input, conv_weight, log_decay, level_weight, grad_out)
 
 
 def back_kernel(
@@ -593,28 +612,8 @@
     vm = pl.BlockSpec(memory_space=pltpu.VMEM)
     params = pltpu.CompilerParams(vmem_limit_bytes=VMEM_LIMIT)
     shape = jax.ShapeDtypeStruct
-    half = (2, BLOCK, channels // 2)
-    fac_rows = (3 * far + 7) // 8 * 8
-    prior, totals = exchange_edges(n, conv_input, log_decay)
-    u_act, slope, end_state, grad_far, factors = pl.pallas_call(
-        functools.partial(front_kernel, far),
-        out_shape=(
-            shape((rows, conv_ch), BF16),
-            shape((rows, conv_ch), F32),
-            shape(half, F32),
-            shape((far,) + half, F32),
-            shape((2, fac_rows, channels // 2), F32),
-        ),
-        in_specs=[vm] * 7,
-        out_specs=(vm,) * 5,
-        scratch_shapes=[
-            pltpu.VMEM((rows + 8, conv_ch), F32),
-            pltpu.VMEM(((1 + far) * rows, 2 * heads), BF16),
-        ],
-        compiler_params=params,
-    )(conv_input, prior, conv_weight, log_decay, level_weight, grad_out, totals)
-    far_states, grad_end, *near = exchange_states(
-        far, end_state, grad_far, factors, log_decay, level_weight, grad_out, u_act
+    prior, u_act, slope, factors, far_states, grad_end, *near = travel(
+        n, conv_input, conv_weight, log_decay, level_weight, grad_out
     )
     mixed, grad_input, grad_level, tail, head, wpart = pl.pallas_call(
         functools.partial(back_kernel, far),

time: 82.8 us -> 75.3 us (0.909)
  Pallas kernels: 79 us -> 71.4 us
    pallas_call x3 -> x1, Pallas kernels: 52.6 us -> 45 us  [travel(): pl.pallas_call(functools.partial(travel_kernel, n, far), out_shape=(shape...]
where the time goes in v3:
time: 75.3 us; the launch traced here: 75 us
  Pallas kernels  71.4 us (95%)
  local copies, waits for them, and re-layouts  2.9 us (4%)
    pallas_call x1, Pallas kernels, travel(): pl.pallas_call(functools.partial(travel_kernel, n, far), out_shape=(shape...  45 us
    pallas_call x1, Pallas kernels, body(): pl.pallas_call(functools.partial(back_kernel, far), out_shape=(shape((row...  13.4 us
    pallas_call x1, Pallas kernels, exchange_finish(): pl.pallas_call(functools.partial(finish_kernel, n, digits), out_shape=(ja...  13.1 us
    dynamic_update_slice x1, local copies, waits for them, and re-layouts, body(): grad_input = lax.dynamic_update_slice(grad_input, tail_rows, (rows - 16, 0))  1.52 us

profile of v3, /device:TPU:0, one launch (start us, length us, event | category | flops | bytes accessed | tf_op | source)
XLA Modules:
  0.0 75.0 jit_solution(3503051447076316726)
XLA Ops:
  0.6 45.0 %shard_map.84 = (bf16[16,2176]{1,0:T(8,128)(2,1)}, bf16[128,2176]{1,0:T(8,128)(2,1)}, f32[128,2176]{1,0:T(8,128)}, f32[2,16,1024]{2,1,0:T(8,128)}, bf16[4,2,64,1...) custom-call(bf16[128,2176]{1,0:T(8,128)(2,1)} %conv_ref.3, ...), custom_call_target="tpu_custom_call" | custom-call | tf_op jit(solution)/shard_map/pallas_call | solution.py:381
  45.6 13.4 %shard_map.85 = (bf16[128,2048]{1,0:T(8,128)(2,1)}, bf16[128,2176]{1,0:T(8,128)(2,1)}, f32[12,32,128]{2,1,0:T(8,128)}, f32[16,2176]{1,0:T(8,128)}, f32[8,2176]{1,0:T(8,128)}, /*index=5*/f32[8,2176]{1,0:T(8,128)}) custom-call(bf16[128,2176]{1,0:T(8,128)(2,1)} %conv_ref.3, bf16[16,2176]{1,0:T(8,128)(2,1)} %get-tuple-element.22.prior_ref, f32[4,2176]{1,0:T(4,128)} %w_ref.5, ...), custom_call_target="tpu_custom_call" | custom-call | tf_op jit(solution)/shard_map/pallas_call | solution.py:618
  59.0 13.1 %shard_map.86 = (bf16[16,2176]{1,0:T(8,128)(2,1)}, f32[4,2176]{1,0:T(4,128)}) custom-call(f32[16,2176]{1,0:T(8,128)} %get-tuple-element.34.tail_ref, f32[8,2176]{1,0:T(8,128)} %get-tuple-element.35.head_ref, f32[8,2176]{1,0:T(8,128)} %get-tuple-element.36.wpart_ref, f32[4,2176]{1,0:T(4,128)} %w_ref.5), custom_call_target="tpu_custom_call" | custom-call | tf_op jit(solution)/shard_map/pallas_call | solution.py:582
  72.1 1.5 %constant_dynamic-update-slice_fusion = bf16[128,2176]{1,0:T(8,128)(2,1)} fusion(bf16[128,2176]{1,0:T(8,128)(2,1)} %get-tuple-element.33, bf16[16,2176]{1,0:T(8,128)(2,1)} %get-tuple-element.37), kind=kLoop, calls=%fused_computation | loop fusion | bytes 139264 | tf_op jit(solution)/shard_map/dynamic_update_slice | solution.py:645
  73.6 1.4 %copy.11 = f32[4,2176]{1,0:T(4,128)} copy(f32[4,2176]{1,0:T(4,128)} %get-tuple-element.47) | data formatting | bytes 69632

commit v4 on v3

--- a/solution.py
+++ b/solution.py
@@ -351,9 +351,147 @@
         far_ref[level, other] = cross_in[level - 1]
 
 
+def back_part(
+    far, conv_ref, prior_ref, w_ref, decay_ref, lw_ref, g_ref, u_ref, slope_ref, fac_ref, far_ref, grad_ref,
+    near_ref, dx_ref, nlev_ref, dbq_ref,
+    mixed_ref, gin_ref, glev_ref, tail_ref, head_ref, wpart_ref,
+    pad, gp, facs, q_s, b2_s, dq_acc, db_acc,
+):
+    rows, channels = g_ref.shape
+    heads = decay_ref.shape[0]
+    taps = w_ref.shape[0]
+    fill_padded(pad, conv_ref, prior_ref)
+    cum = running_decay(decay_ref)
+    base = [jnp.exp(cum[rows - 1 : rows] - cum), jnp.exp(cum)]
+    base += [lw_ref[2 + level].T * level_scale(2 + level) for level in range(far)]
+    for idx, value in enumerate(base):
+        facs[idx * rows : (idx + 1) * rows, :] = jnp.concatenate(split2(value), axis=1)
+    bq = u_ref[:, channels:]
+    q_s[...] = bq[:, BLOCK:]
+    b2_s[...] = jnp.concatenate([bq[:, :BLOCK]] * 2, axis=1)
+    dq_acc[...] = jnp.zeros_like(dq_acc)
+    db_acc[...] = jnp.zeros_like(db_acc)
+    glev_ref[...] = jnp.zeros_like(glev_ref)
+    glev_ref[0:2] = nlev_ref[...]
+    per_half = channels // 2 // LANES
+
+    @pl.loop(0, channels // LANES)
+    def _(j):
+        cols = pl.ds(pl.multiple_of(j * LANES, LANES), LANES)
+        side = j // per_half
+        part = pl.ds(pl.multiple_of((j % per_half) * LANES, LANES), LANES)
+        x = u_ref[:, cols]
+        g = g_ref[:, cols].astype(F32)
+        spread = dot(facs[...], one_hot(2 * heads, heads, 2 * j, LANES, BLOCK))
+
+        def fac(idx):
+            return spread[idx * rows : (idx + 1) * rows]
+
+        mixed = near_ref[:, cols]
+        products, inner, states = [], [], []
+        for level in range(far):
+            state = far_ref[level, side, :, part]
+            scale = fac(1) * fac_ref[side, 2 * far + level : 2 * far + level + 1, part]
+            out = dot(q_s[...], state) * scale
+            weight = fac(2 + level)
+            mixed = mixed + weight * out
+            products.append(g * out)
+            inner.append((g * weight * scale).astype(BF16))
+            states.append(state)
+        mixed_ref[:, cols] = mixed.astype(BF16)
+        dq_acc[...] += dot_nt(jnp.concatenate(inner, axis=1), jnp.concatenate(states, axis=1))
+        pick = head_pick(heads, j)
+        for level, product in enumerate(products):
+            sums = dot_nt(pick, jnp.concatenate(split2(product), axis=1))
+            glev_ref[2 + level] += sums * level_scale(2 + level)
+
+        grad = grad_ref[side, :, part]
+        hi, lo = split2(grad)
+        key_decay = fac(0)
+        dx = dx_ref[:, cols] + key_decay * dot(b2_s[...], jnp.concatenate([hi, lo], axis=0))
+        db_acc[...] += dot_nt((x.astype(F32) * key_decay).astype(BF16), hi)
+        gp[0:rows, cols] = dx * slope_ref[:, cols]
+
+    dbq = dbq_ref[...] + jnp.concatenate([db_acc[...], dq_acc[...]], axis=1)
+    gp[0:rows, channels:] = dbq * slope_ref[:, channels:]
+    gp[rows:, :] = jnp.zeros((8, gp.shape[1]), F32)
+    head_ref[...] = gp[0:8, :]
+
+    @pl.loop(0, gp.shape[1] // LANES)
+    def _(j):
+        cols = pl.ds(pl.multiple_of(j * LANES, LANES), LANES)
+        grad = gp[0:rows, cols]
+        acc = w_ref[taps - 1 : taps, cols] * grad
+        sums = []
+        for k in range(taps):
+            shift = taps - 1 - k
+            if shift:
+                acc = acc + w_ref[k : k + 1, cols] * gp[shift : shift + rows, cols]
+            sums.append(jnp.sum(pad[8 - shift : 8 - shift + rows, cols] * grad, axis=0, keepdims=True))
+        gin_ref[:, cols] = acc.astype(BF16)
+        tail_ref[:, cols] = acc[rows - 16 :]
+        sums.append(jnp.zeros((8 - taps, LANES), F32))
+        wpart_ref[:, cols] = jnp.concatenate(sums, axis=0)
+
+
+def finish_part(digits, n, tail_ref, head_ref, wpart_ref, w_ref, gin_ref, wsum_ref, lead, nxt, acc, slots, hs, hr, send, recv):
+    me = lax.axis_index("ctx")
+    taps = w_ref.shape[0]
+    channels = w_ref.shape[1]
+    width = acc.shape[2]
+    skip = channels - width
+
+    def packed(rows):
+        return jnp.concatenate([rows[:4, :width], rows[:4, skip:]], axis=0)
+
+    def unpacked(value):
+        return jnp.concatenate([value[:4, :skip], value[4:]], axis=1)
+
+    lead[...] = packed(head_ref[...])
+    acc[0] = packed(wpart_ref[...])
+    before = lax.rem(me + n - 1, n)
+    plan = []
+    for shift, size in digits:
+        digit = (me >> shift) & (size - 1)
+        plan.append((digit, [me ^ (d << shift) for d in range(1, size)]))
+    row_copy = pltpu.make_async_remote_copy(lead, nxt, hs, hr, at(before), MESH)
+    row_copy.start()
+    for stage, (digit, peers) in enumerate(plan):
+        copies = []
+        for d, peer in enumerate(peers):
+            copy = pltpu.make_async_remote_copy(
+                acc.at[stage], slots.at[stage, d], send.at[stage, d], recv.at[stage, d], at(peer), MESH
+            )
+            copy.start()
+            copies.append(copy)
+        if stage == 0:
+            row_copy.wait()
+            keep = jnp.where(me < n - 1, 1.0, 0.0)
+            rows = unpacked(nxt[...]) * keep
+            blank = jnp.zeros((8, channels), F32)
+            joined = jnp.concatenate([blank, rows, blank[:4]], axis=0)
+            fix = blank
+            for k in range(taps - 1):
+                shift = taps - 1 - k
+                fix = fix + w_ref[k : k + 1, :] * joined[shift : shift + 8]
+            gin_ref[gin_ref.shape[0] - 16 :, :] = (tail_ref[...] + jnp.concatenate([jnp.zeros_like(fix), fix], axis=0)).astype(BF16)
+        for copy in copies:
+            copy.wait()
+        size = len(peers) + 1
+        have = [acc[stage]] + [slots[stage, d] for d in range(size - 1)]
+        if size == 2:
+            total = have[0] + have[1]
+        else:
+            total = (have[0] + have[1]) + (have[2] + have[3])
+        acc[stage + 1] = total
+    wsum_ref[...] = unpacked(acc[len(plan)])[:taps]
+
+
 def travel_kernel(
-    n, far, conv_ref, w_ref, decay_ref, lw_ref, g_ref,
-    prior_ref, u_ref, slope_ref, fac_ref, far_ref, grad_ref, mixed_ref, dx_ref, glev_ref, dbq_ref,
+    n, far, digits, conv_ref, w_ref, decay_ref, lw_ref, g_ref,
+    mixed_ref, gin_ref, glev_ref, wsum_ref,
+    prior_ref, u_ref, slope_ref, fac_ref, far_ref, grad_ref, near_ref, dx_ref, nlev_ref, dbq_ref,
+    tail, head, wpart, gp, bfacs, q_s, b2_s, dq_acc, db_acc, lead, nxt, acc, tslots, hs, hr, tsend, trecv,
     totals, mine, slots, rows, send, recv, rsend, rrecv, pad, facs, end, gf, *rest,
 ):
     finish = start_edges(n, conv_ref, decay_ref, prior_ref, totals, mine, slots, rows, send, recv, rsend, rrecv)
@@ -363,8 +501,15 @@
     )
     fenwick_part(
         far, end, gf, fac_ref, decay_ref, lw_ref, g_ref, u_ref,
-        far_ref, grad_ref, mixed_ref, dx_ref, glev_ref, dbq_ref, *rest,
+        far_ref, grad_ref, near_ref, dx_ref, nlev_ref, dbq_ref, *rest,
     )
+    back_part(
+        far, conv_ref, prior_ref, w_ref, decay_ref, lw_ref, g_ref, u_ref, slope_ref, fac_ref, far_ref, grad_ref,
+        near_ref, dx_ref, nlev_ref, dbq_ref,
+        mixed_ref, gin_ref, glev_ref, tail, head, wpart,
+        pad, gp, bfacs, q_s, b2_s, dq_acc, db_acc,
+    )
+    finish_part(digits, n, tail, head, wpart, w_ref, gin_ref, wsum_ref, lead, nxt, acc, tslots, hs, hr, tsend, trecv)
 
 
 def travel(n, conv_input, conv_weight, log_decay, level_weight, grad_out):
@@ -377,24 +522,47 @@
     stack = (far - 1,) + piece
     fac_rows = (3 * far + 7) // 8 * 8
     shape = jax.ShapeDtypeStruct
+    digits = [(shift, 1 << min(2, far - shift)) for shift in range(0, far, 2)]
+    width = (conv_ch // LANES + 1) // 2 * LANES
     vm = pl.BlockSpec(memory_space=pltpu.VMEM)
     return pl.pallas_call(
-        functools.partial(travel_kernel, n, far),
+        functools.partial(travel_kernel, n, far, digits),
         out_shape=(
-            shape((16, conv_ch), BF16),
+            shape((rows, channels), BF16),
             shape((rows, conv_ch), BF16),
-            shape((rows, conv_ch), F32),
-            shape((2, fac_rows, channels // 2), F32),
-            shape((far,) + half, BF16),
-            shape(half, F32),
-            shape((rows, channels), F32),
-            shape((rows, channels), F32),
-            shape((2, heads, rows), F32),
-            shape((rows, LANES), F32),
+            shape(level_weight.shape, F32),
+            shape(conv_weight.shape, F32),
         ),
         in_specs=[vm] * 5,
-        out_specs=(vm,) * 10,
+        out_specs=(vm,) * 4,
         scratch_shapes=[
+            pltpu.VMEM((16, conv_ch), BF16),
+            pltpu.VMEM((rows, conv_ch), BF16),
+            pltpu.VMEM((rows, conv_ch), F32),
+            pltpu.VMEM((2, fac_rows, channels // 2), F32),
+            pltpu.VMEM((far,) + half, BF16),
+            pltpu.VMEM(half, F32),
+            pltpu.VMEM((rows, channels), F32),
+            pltpu.VMEM((rows, channels), F32),
+            pltpu.VMEM((2, heads, rows), F32),
+            pltpu.VMEM((rows, LANES), F32),
+            pltpu.VMEM((16, conv_ch), F32),
+            pltpu.VMEM((8, conv_ch), F32),
+            pltpu.VMEM((8, conv_ch), F32),
+            pltpu.VMEM((rows + 8, conv_ch), F32),
+            pltpu.VMEM(((2 + far) * rows, 2 * heads), BF16),
+            pltpu.VMEM((rows, BLOCK), BF16),
+            pltpu.VMEM((rows, 2 * BLOCK), BF16),
+            pltpu.VMEM((rows, BLOCK), F32),
+            pltpu.VMEM((rows, BLOCK), F32),
+            pltpu.VMEM((8, width), F32),
+            pltpu.VMEM((8, width), F32),
+            pltpu.VMEM((len(digits) + 1, 8, width), F32),
+            pltpu.VMEM((len(digits), 3, 8, width), F32),
+            pltpu.SemaphoreType.DMA,
+            pltpu.SemaphoreType.DMA,
+            pltpu.SemaphoreType.DMA((len(digits), 3)),
+            pltpu.SemaphoreType.DMA((len(digits), 3)),
             pltpu.VMEM((n, 8, LANES), F32),
             pltpu.VMEM((8, LANES), F32),
             pltpu.VMEM((n - 1, 8, LANES), F32),
@@ -431,222 +599,10 @@
     )(conv_input, conv_weight, log_decay, level_weight, grad_out)
 
 
-def back_kernel(
-    far, conv_ref, prior_ref, w_ref, decay_ref, lw_ref, g_ref, u_ref, slope_ref, fac_ref, far_ref, grad_ref,
-    near_ref, dx_ref, nlev_ref, dbq_ref,
-    mixed_ref, gin_ref, glev_ref, tail_ref, head_ref, wpart_ref,
-    pad, gp, facs, q_s, b2_s, dq_acc, db_acc,
-):
-    rows, channels = g_ref.shape
-    heads = decay_ref.shape[0]
-    taps = w_ref.shape[0]
-    fill_padded(pad, conv_ref, prior_ref)
-    cum = running_decay(decay_ref)
-    base = [jnp.exp(cum[rows - 1 : rows] - cum), jnp.exp(cum)]
-    base += [lw_ref[2 + level].T * level_scale(2 + level) for level in range(far)]
-    for idx, value in enumerate(base):
-        facs[idx * rows : (idx + 1) * rows, :] = jnp.concatenate(split2(value), axis=1)
-    bq = u_ref[:, channels:]
-    q_s[...] = bq[:, BLOCK:]
-    b2_s[...] = jnp.concatenate([bq[:, :BLOCK]] * 2, axis=1)
-    dq_acc[...] = jnp.zeros_like(dq_acc)
-    db_acc[...] = jnp.zeros_like(db_acc)
-    glev_ref[...] = jnp.zeros_like(glev_ref)
-    glev_ref[0:2] = nlev_ref[...]
-    per_half = channels // 2 // LANES
-
-    @pl.loop(0, channels // LANES)
-    def _(j):
-        cols = pl.ds(pl.multiple_of(j * LANES, LANES), LANES)
-        side = j // per_half
-        part = pl.ds(pl.multiple_of((j % per_half) * LANES, LANES), LANES)
-        x = u_ref[:, cols]
-        g = g_ref[:, cols].astype(F32)
-        spread = dot(facs[...], one_hot(2 * heads, heads, 2 * j, LANES, BLOCK))
-
-        def fac(idx):
-            return spread[idx * rows : (idx + 1) * rows]
-
-        mixed = near_ref[:, cols]
-        products, inner, states = [], [], []
-        for level in range(far):
-            state = far_ref[level, side, :, part]
-            scale = fac(1) * fac_ref[side, 2 * far + level : 2 * far + level + 1, part]
-            out = dot(q_s[...], state) * scale
-            weight = fac(2 + level)
-            mixed = mixed + weight * out
-            products.append(g * out)
-            inner.append((g * weight * scale).astype(BF16))
-            states.append(state)
-        mixed_ref[:, cols] = mixed.astype(BF16)
-        dq_acc[...] += dot_nt(jnp.concatenate(inner, axis=1), jnp.concatenate(states, axis=1))
-        pick = head_pick(heads, j)
-        for level, product in enumerate(products):
-            sums = dot_nt(pick, jnp.concatenate(split2(product), axis=1))
-            glev_ref[2 + level] += sums * level_scale(2 + level)
-
-        grad = grad_ref[side, :, part]
-        hi, lo = split2(grad)
-        key_decay = fac(0)
-        dx = dx_ref[:, cols] + key_decay * dot(b2_s[...], jnp.concatenate([hi, lo], axis=0))
-        db_acc[...] += dot_nt((x.astype(F32) * key_decay).astype(BF16), hi)
-        gp[0:rows, cols] = dx * slope_ref[:, cols]
-
-    dbq = dbq_ref[...] + jnp.concatenate([db_acc[...], dq_acc[...]], axis=1)
-    gp[0:rows, channels:] = dbq * slope_ref[:, channels:]
-    gp[rows:, :] = jnp.zeros((8, gp.shape[1]), F32)
-    head_ref[...] = gp[0:8, :]
-
-    @pl.loop(0, gp.shape[1] // LANES)
-    def _(j):
-        cols = pl.ds(pl.multiple_of(j * LANES, LANES), LANES)
-        grad = gp[0:rows, cols]
-        acc = w_ref[taps - 1 : taps, cols] * grad
-        sums = []
-        for k in range(taps):
-            shift = taps - 1 - k
-            if shift:
-                acc = acc + w_ref[k : k + 1, cols] * gp[shift : shift + rows, cols]
-            sums.append(jnp.sum(pad[8 - shift : 8 - shift + rows, cols] * grad, axis=0, keepdims=True))
-        gin_ref[:, cols] = acc.astype(BF16)
-        tail_ref[:, cols] = acc[rows - 16 :]
-        sums.append(jnp.zeros((8 - taps, LANES), F32))
-        wpart_ref[:, cols] = jnp.concatenate(sums, axis=0)
-
-
-def finish_kernel(n, digits, tail_ref, head_ref, wpart_ref, w_ref, out_ref, wsum_ref, lead, nxt, acc, slots, hs, hr, send, recv):
-    me = lax.axis_index("ctx")
-    taps = w_ref.shape[0]
-    channels = w_ref.shape[1]
-    width = acc.shape[2]
-    skip = channels - width
-
-    def packed(rows):
-        return jnp.concatenate([rows[:4, :width], rows[:4, skip:]], axis=0)
-
-    def unpacked(value):
-        return jnp.concatenate([value[:4, :skip], value[4:]], axis=1)
-
-    lead[...] = packed(head_ref[...])
-    acc[0] = packed(wpart_ref[...])
-    before, after = lax.rem(me + n - 1, n), lax.rem(me + 1, n)
-    plan = []
-    for shift, size in digits:
-        digit = (me >> shift) & (size - 1)
-        plan.append((digit, [me ^ (d << shift) for d in range(1, size)]))
-    greet([at(before), at(after)] + [at(p) for _, peers in plan for p in peers])
-    row_copy = pltpu.make_async_remote_copy(lead, nxt, hs, hr, at(before), MESH)
-    row_copy.start()
-    for stage, (digit, peers) in enumerate(plan):
-        copies = []
-        for d, peer in enumerate(peers):
-            copy = pltpu.make_async_remote_copy(
-                acc.at[stage], slots.at[stage, d], send.at[stage, d], recv.at[stage, d], at(peer), MESH
-            )
-            copy.start()
-            copies.append(copy)
-        if stage == 0:
-            row_copy.wait()
-            keep = jnp.where(me < n - 1, 1.0, 0.0)
-            rows = unpacked(nxt[...]) * keep
-            blank = jnp.zeros((8, channels), F32)
-            joined = jnp.concatenate([blank, rows, blank[:4]], axis=0)
-            fix = blank
-            for k in range(taps - 1):
-                shift = taps - 1 - k
-                fix = fix + w_ref[k : k + 1, :] * joined[shift : shift + 8]
-            out_ref[...] = (tail_ref[...] + jnp.concatenate([jnp.zeros_like(fix), fix], axis=0)).astype(BF16)
-        for copy in copies:
-            copy.wait()
-        size = len(peers) + 1
-        have = [acc[stage]] + [slots[stage, d] for d in range(size - 1)]
-        if size == 2:
-            total = have[0] + have[1]
-        else:
-            total = (have[0] + have[1]) + (have[2] + have[3])
-        acc[stage + 1] = total
-    wsum_ref[...] = unpacked(acc[len(plan)])[:taps]
-
-
-def exchange_finish(n, tail, head, wpart, conv_weight):
-    far = n.bit_length() - 1
-    digits = []
-    shift = 0
-    while shift < far:
-        bits = min(2, far - shift)
-        digits.append((shift, 1 << bits))
-        shift += bits
-    channels = tail.shape[1]
-    width = (channels // LANES + 1) // 2 * LANES
-    vm = pl.BlockSpec(memory_space=pltpu.VMEM)
-    return pl.pallas_call(
-        functools.partial(finish_kernel, n, digits),
-        out_shape=(
-            jax.ShapeDtypeStruct((16, channels), BF16),
-            jax.ShapeDtypeStruct(conv_weight.shape, F32),
-        ),
-        in_specs=[vm] * 4,
-        out_specs=(vm, vm),
-        scratch_shapes=[
-            pltpu.VMEM((8, width), F32),
-            pltpu.VMEM((8, width), F32),
-            pltpu.VMEM((len(digits) + 1, 8, width), F32),
-            pltpu.VMEM((len(digits), 3, 8, width), F32),
-            pltpu.SemaphoreType.DMA,
-            pltpu.SemaphoreType.DMA,
-            pltpu.SemaphoreType.DMA((len(digits), 3)),
-            pltpu.SemaphoreType.DMA((len(digits), 3)),
-        ],
-        compiler_params=pltpu.CompilerParams(
-            collective_id=2, has_side_effects=True, vmem_limit_bytes=VMEM_LIMIT
-        ),
-    )(tail, head, wpart, conv_weight)
-
-
-def body(conv_input, conv_weight, log_decay, level_weight, grad_out):
-    n = lax.axis_size("ctx")
-    far = n.bit_length() - 1
-    rows, conv_ch = conv_input.shape
-    channels = grad_out.shape[1]
-    heads = log_decay.shape[0]
-    vm = pl.BlockSpec(memory_space=pltpu.VMEM)
-    params = pltpu.CompilerParams(vmem_limit_bytes=VMEM_LIMIT)
-    shape = jax.ShapeDtypeStruct
-    prior, u_act, slope, factors, far_states, grad_end, *near = travel(
-        n, conv_input, conv_weight, log_decay, level_weight, grad_out
-    )
-    mixed, grad_input, grad_level, tail, head, wpart = pl.pallas_call(
-        functools.partial(back_kernel, far),
-        out_shape=(
-            shape((rows, channels), BF16),
-            shape((rows, conv_ch), BF16),
-            shape(level_weight.shape, F32),
-            shape((16, conv_ch), F32),
-            shape((8, conv_ch), F32),
-            shape((8, conv_ch), F32),
-        ),
-        in_specs=[vm] * 15,
-        out_specs=(vm,) * 6,
-        scratch_shapes=[
-            pltpu.VMEM((rows + 8, conv_ch), F32),
-            pltpu.VMEM((rows + 8, conv_ch), F32),
-            pltpu.VMEM(((2 + far) * rows, 2 * heads), BF16),
-            pltpu.VMEM((rows, BLOCK), BF16),
-            pltpu.VMEM((rows, 2 * BLOCK), BF16),
-            pltpu.VMEM((rows, BLOCK), F32),
-            pltpu.VMEM((rows, BLOCK), F32),
-        ],
-        compiler_params=params,
-    )(
-        conv_input, prior, conv_weight, log_decay, level_weight, grad_out,
-        u_act, slope, factors, far_states, grad_end, *near,
-    )
-    tail_rows, weight_grad = exchange_finish(n, tail, head, wpart, conv_weight)
-    grad_input = lax.dynamic_update_slice(grad_input, tail_rows, (rows - 16, 0))
-    return (mixed, grad_input, grad_level, weight_grad)
-
-
 def solution(mesh):
+    def body(*args):
+        return travel(lax.axis_size("ctx"), *args)
+
     in_specs = (
         P(("groups", "ctx"), None),
         P(),

time: 75.3 us -> 68.3 us (0.907)
  Pallas kernels: 71.4 us -> 62.9 us
  local copies, waits for them, and re-layouts: 2.9 us -> 4.44 us
    pallas_call x3 -> x1, Pallas kernels: 71.4 us -> 62.9 us  [travel(): pl.pallas_call(functools.partial(travel_kernel, n, far, digits), out_shap...]
    unnamed x1 -> x10, local copies, waits for them, and re-layouts: 1.38 us -> 4.44 us
    dynamic_update_slice x1 -> x0, local copies, waits for them, and re-layouts: 1.52 us -> none  [body(): grad_input = lax.dynamic_update_slice(grad_input, tail_rows, (rows - 16, 0))]
where the time goes in v4:
time: 68.3 us; the launch traced here: 68 us
  Pallas kernels  62.9 us (92%)
  local copies, waits for them, and re-layouts  4.44 us (7%)
    pallas_call x1, Pallas kernels, travel(): pl.pallas_call(functools.partial(travel_kernel, n, far, digits), out_shap...  62.9 us
    unnamed x10, local copies, waits for them, and re-layouts  4.44 us

profile of v4, /device:TPU:0, one launch (start us, length us, event | category | flops | bytes accessed | tf_op | source)
XLA Modules:
  0.0 68.0 jit_solution(7303609629933932612)
XLA Ops:
  0.6 62.9 %shard_map.84 = (bf16[128,2048]{1,0:T(8,128)(2,1)}, bf16[128,2176]{1,0:T(8,128)(2,1)}, f32[12,32,128]{2,1,0:T(8,128)}, f32[4,2176]{1,0:T(4,128)}) custom-call(bf16[128,2176]{1,0:T(8,128)(2,1)} %conv_ref.1, f32[4,2176]{1,0:T(4,128)} %w_ref.1, f32[32,128]{1,0:T(8,128)} %decay_ref.1, f32[12,32,128]{2,1,0:T(8,128)} %lw_ref.1, bf16[128,2048]{1,0:T(8,128)(2,1)} %g_ref.1), custom_call_target="tpu_custom_call" | custom-call | tf_op jit(solution)/shard_map/pallas_call | solution.py:528
  63.6 0.0 copy-start
  63.6 1.9 %copy.13 = bf16[128,2048]{1,0:T(8,128)(2,1)} copy(bf16[128,2048]{1,0:T(8,128)(2,1)} %get-tuple-element.8) | data formatting | bytes 1048576
  65.5 0.0 copy-done
  65.5 0.0 copy-start.1
  65.5 0.8 %copy.14 = bf16[128,2176]{1,0:T(8,128)(2,1)} copy(bf16[128,2176]{1,0:T(8,128)(2,1)S(1)} %copy-done) | data formatting | bytes 1114112
  66.3 0.3 copy-done.1
  66.7 0.0 copy-start.2
  66.7 0.7 copy.15
  67.3 0.1 copy-done.2
  67.4 0.6 copy.16
Async XLA Ops:
  63.6 2.0 %copy-start = (bf16[128,2176]{1,0:T(8,128)(2,1)S(1)}, bf16[128,2176]{1,0:T(8,128)(2,1)}, u32[]{:S(2)}) copy-start(bf16[128,2176]{1,0:T(8,128)(2,1)} %get-tuple-element.9) | copy-start | bytes 1671172
  65.5 1.1 %copy-start.1 = (f32[12,32,128]{2,1,0:T(8,128)S(1)}, f32[12,32,128]{2,1,0:T(8,128)}, u32[]{:S(2)}) copy-start(f32[12,32,128]{2,1,0:T(8,128)} %get-tuple-element.10) | copy-start | bytes 589828
  66.7 0.8 %copy-start.2 = (f32[4,2176]{1,0:T(4,128)S(1)}, f32[4,2176]{1,0:T(4,128)}, u32[]{:S(2)}) copy-start(f32[4,2176]{1,0:T(4,128)} %get-tuple-element.11) | copy-start | bytes 104452
